TPU v7x, 32 devices: a whole 2x2x4 slice. The times are simulated.
32 devices in a mesh: dp: 16 (over z, y, x), tensor: 2 (over core).
Axes of the slice: x: 2, y: 2, z: 4, core: 2. Of those that a mesh axis runs over, the one named last changes fastest.
Arguments:
- tokens: bfloat16 [4096, 2048], P(('dp', 'tensor')), may hold values from -6 to 6
- norm1_gain: bfloat16 [2048], P('dp'), may hold values from 0.099609375 to 1.8984375
- qkv_weight: bfloat16 [2048, 3, 2048], P('dp', None, 'tensor'), may hold values from -0.125 to 0.125
- out_weight: bfloat16 [2048, 2048], P('dp', 'tensor'), may hold values from -0.5 to 0.5
- norm2_gain: bfloat16 [2048], P('dp'), may hold values from 0.099609375 to 1.8984375
- gate_up_weight: bfloat16 [2048, 2, 5632], P('dp', None, 'tensor'), may hold values from -0.125 to 0.125
- down_weight: bfloat16 [2048, 5632], P('dp', 'tensor'), may hold values from -0.078125 to 0.078125
- doc_lengths: int32 [16, 8], P('dp'), may hold values from 1 to 128, 256 in all within a row
- cotangent: bfloat16 [4096, 2048], P(('dp', 'tensor')), may hold values from -6 to 6
Outputs:
- output: bfloat16 [4096, 2048], P(('dp', 'tensor'))
- input_grad: bfloat16 [4096, 2048], P(('dp', 'tensor'))
- norm1_gain_grad: float32 [2048], P('dp')
- qkv_grad: float32 [2048, 3, 2048], P('dp', None, 'tensor')
- out_grad: float32 [2048, 2048], P('dp', 'tensor')
- norm2_gain_grad: float32 [2048], P('dp')
- gate_up_grad: float32 [2048, 2, 5632], P('dp', None, 'tensor')
- down_grad: float32 [2048, 5632], P('dp', 'tensor')
Inputs may be any that keep to these rules, and one draw needn't show every extreme that they name: `doc_lengths`: in every packed row the 8 lengths sum to 256, and the longest is 128.
All inputs are finite; a program needn't handle non-finite values.
Results may differ from a plain program's by a relative error of at most 0.014.
Values may be sent and summed in bfloat16 or wider, within the bound.
No kernel may reach another device: no remote copies, remote signals or barrier semaphores. Data moves between devices by JAX's collectives and lax.ppermute only.
A program may use at most 256 MiB of HBM per device.

v0:
```python
import functools
import math

import jax
import jax.numpy as jnp
from jax import lax
from jax.experimental import pallas as pl
from jax.experimental.pallas import tpu as pltpu
from jax.sharding import PartitionSpec as P

HEAD_DIM = 128
EPS_NORM = 1e-05
MASKED_SCORE = -1e30
GROUP = 4
X, Y = 1, 2
BF = jnp.bfloat16
F32 = jnp.float32
VMEM_LIMIT = 60 * 2**20


def over_dp(x, bit):
    size = lax.axis_size("dp")
    return lax.ppermute(x, "dp", [(i, i ^ bit) for i in range(size)])


def over_cores(x):
    return lax.ppermute(x, "tensor", [(0, 1), (1, 0)])


def groups():
    size = lax.axis_size("dp")
    return [list(range(first, first + GROUP)) for first in range(0, size, GROUP)]


def ring():
    count = lax.axis_size("dp") // GROUP
    return [*range(0, count, 2)][:1] + [*range(1, count, 2)] + [*range(2, count, 2)][::-1]


def over_ring(x):
    order = ring()
    pairs = zip(order, order[1:] + order[:1])
    return lax.ppermute(
        x, "dp", [(GROUP * a + i, GROUP * b + i) for a, b in pairs for i in range(GROUP)]
    )


def after(x, *others):
    return lax.optimization_barrier((x, *others))[0]


def after_all(arrays, *others):
    return list(lax.optimization_barrier((*arrays, *others)))[: len(arrays)]


def with_other_core(blocks):
    return [array for block in blocks for array in (block, over_cores(block))]


def part_of(pieces, first, rows):
    moves = [(i, first, i // 2, (i % 2) * rows, rows) for i in range(len(pieces))]
    return pieces, tuple(moves)


def gather(own):
    x, y = over_dp(own, X), over_dp(own, Y)
    return [own, x, y, over_dp(x, Y)]


def plus(base, more):
    return (base.astype(F32) + more.astype(F32)).astype(BF)


def both_cores(own, other):
    other = over_cores(other)
    return [plus(own[step], other[step]) for step in range(GROUP)]


def reduce_first(blocks):
    own, x, y, xy = blocks
    return [own, plus(x, over_dp(xy, Y)), y]


def reduce_last(own, x, y):
    terms = [own, over_dp(x, X), over_dp(y, Y)]
    return sum(term.astype(F32) for term in terms)


def swap_members(blocks):
    return lax.all_to_all(
        blocks, "dp", split_axis=0, concat_axis=0, tiled=True, axis_index_groups=groups()
    )


def outer_gather(block):
    blocks = [block]
    for _ in ring()[1:]:
        blocks.append(over_ring(blocks[-1]))
    return blocks


def outer_reduce(part):
    chunks = part.reshape(-1, GROUP, *part.shape[1:])
    got = [over_ring(chunks[1])]
    for k in range(2, chunks.shape[0]):
        got.append(over_ring(plus(got[-1], chunks[k])))
    return got, plus(got[-1], chunks[0])


def dot(left, right, left_dim, right_dim):
    return lax.dot_general(
        left, right, (((left_dim,), (right_dim,)), ((), ())), preferred_element_type=F32
    )


def moves_of(moves, piece_refs, held, sems):
    return [
        (
            step,
            pltpu.make_async_copy(
                piece_refs[index].at[pl.ds(source, rows)],
                held.at[step, pl.ds(row, rows)],
                sems.at[index],
            ),
        )
        for index, source, step, row, rows in moves
    ]


def fetch(moves, piece_refs, held, sems, step):
    copies = moves_of(moves, piece_refs, held, sems)

    @pl.when(step == 0)
    def _():
        for _, copy in copies:
            copy.start()

    for index in range(GROUP):

        @pl.when(step == index)
        def _():
            for at, copy in copies:
                if at == index:
                    copy.wait()


def turned(values, cosine, sine):
    return values * cosine + pltpu.roll(values, HEAD_DIM // 2, 1) * sine


def probabilities(queries, keys, mask):
    scores = dot(queries, keys, 1, 1) * (HEAD_DIM**-0.5)
    scores = jnp.where(mask > 0, scores, MASKED_SCORE)
    exps = jnp.exp(scores - jnp.max(scores, axis=1, keepdims=True))
    return exps / jnp.sum(exps, axis=1, keepdims=True)


def params():
    return pltpu.CompilerParams(
        dimension_semantics=("arbitrary",), vmem_limit_bytes=VMEM_LIMIT
    )


def whole(array):
    return pl.BlockSpec(array.shape, lambda step, places: (0,) * array.ndim)


def stepped(*block):
    return pl.BlockSpec((1, *block), lambda step, places: (step,) + (0,) * len(block))


ANYWHERE = pl.BlockSpec(memory_space=pl.ANY)


def up_to_lanes(columns):
    return -(-columns // 128) * 128


def fetch_weights(refs, held, sems, step):
    blocks = refs[0].shape[0]
    copies = [
        pltpu.make_async_copy(ref, held.at[pl.ds(i * blocks, blocks)], sems.at[i])
        for i, ref in enumerate(refs)
    ]

    @pl.when(step == 0)
    def _():
        for copy in copies:
            copy.start()

    def wait():
        @pl.when(step == 0)
        def _():
            for copy in copies:
                copy.wait()

    return wait


def head_weights(held, rows):
    owners, _, columns = held.shape
    cut = columns // 4 * 3
    return (
        held[:, :rows, :cut].reshape(owners * rows, cut),
        held[:, :rows, cut:].reshape(owners * rows, columns - cut),
    )


def heads_of(width):
    return [(i, i + HEAD_DIM) for i in range(0, width, HEAD_DIM)]


def attend_kernel(moves, shard_rows, outer, places, cosine, sine, mask, *refs):
    weights, refs = refs[:outer], refs[outer:]
    count = len(moves)
    pieces, refs = refs[:count], refs[count:]
    a_own, a_other, mixed_ref, q_ref, k_ref, v_ref, held, weight, sems, weight_sems = refs
    step = pl.program_id(0)
    wait = fetch_weights(weights, weight, weight_sems, step)
    fetch(moves, pieces, held, sems, step)
    wait()
    qkv_w, out_w = head_weights(weight, shard_rows)
    projected = dot(held[step], qkv_w, 1, 0)
    width = out_w.shape[1]
    for low, high in heads_of(width):
        queries = turned(projected[:, low:high], cosine[0], sine[0]).astype(BF)
        keys = turned(projected[:, width + low : width + high], cosine[0], sine[0]).astype(BF)
        values = projected[:, 2 * width + low : 2 * width + high].astype(BF)
        q_ref[0, :, low:high], k_ref[0, :, low:high], v_ref[0, :, low:high] = queries, keys, values
        probs = probabilities(queries, keys, mask[0]).astype(BF)
        mixed_ref[0, :, low:high] = dot(probs, values, 1, 0).astype(BF)
    mixed = mixed_ref[0]
    attn = dot(mixed, out_w, 1, 1).astype(BF)
    half = attn.shape[0] // 2
    a_own[0], a_other[0] = attn[:half], attn[half:]


def row_specs(tokens):
    return [stepped(tokens, HEAD_DIM), stepped(tokens, HEAD_DIM), stepped(tokens, tokens)]


def attend(places, rows_one, weights, shard_rows, cosine, sine, mask):
    arrays, moves = rows_one
    tokens, width = mask.shape[1], arrays[0].shape[1]
    half = tokens // 2
    outer = len(weights)
    made = [jax.ShapeDtypeStruct((GROUP, half, width), BF)] * 2
    own = weights[0].shape[2] // 4
    made += [jax.ShapeDtypeStruct((GROUP, tokens, own), BF)] * 4
    return pl.pallas_call(
        functools.partial(attend_kernel, moves, shard_rows, outer),
        grid_spec=pltpu.PrefetchScalarGridSpec(
            num_scalar_prefetch=1,
            grid=(GROUP,),
            in_specs=row_specs(tokens) + [ANYWHERE] * (outer + len(arrays)),
            out_specs=[stepped(half, width)] * 2 + [stepped(tokens, own)] * 4,
            scratch_shapes=[
                pltpu.VMEM((GROUP, tokens, width), BF),
                pltpu.VMEM((outer * GROUP, *weights[0].shape[1:]), BF),
                pltpu.SemaphoreType.DMA((len(arrays),)),
                pltpu.SemaphoreType.DMA((outer,)),
            ],
        ),
        out_shape=made,
        compiler_params=params(),
        cost_estimate=pl.CostEstimate(
            flops=2 * GROUP * tokens * (width * 4 + 2 * tokens) * own,
            bytes_accessed=4 * GROUP * tokens * width,
            transcendentals=GROUP * tokens * tokens,
        ),
        name="attend",
    )(places, cosine, sine, mask, *weights, *arrays)


def feed_kernel(moves, cot_moves, outer, places, *refs):
    weights, refs = refs[:outer], refs[outer:]
    count, cot_count = len(moves), len(cot_moves)
    pieces, cots, refs = refs[:count], refs[count : count + cot_count], refs[count + cot_count :]
    m_own, m_other, y_own, y_other, hidden_ref, grads_ref, *refs = refs
    held, held_cot, weight, sems, cot_sems, weight_sems = refs
    step = pl.program_id(0)
    wait = fetch_weights(weights, weight, weight_sems, step)
    fetch(moves, pieces, held, sems, step)
    fetch(cot_moves, cots, held_cot, cot_sems, step)
    wait()
    width = held.shape[2]
    own = grads_ref.shape[2] // 2
    pair_w = weight[:, :, : 2 * own].reshape(width, 2 * own)
    down_w = weight[:, :, 2 * own : 3 * own].reshape(width, own)
    rows = held[step]
    half = rows.shape[0] // 2
    both = dot(rows, pair_w, 1, 0)
    gate, upper = both[:, :own], both[:, own:]
    grad_hidden = dot(held_cot[step], down_w, 1, 0)
    sigma = 1.0 / (1.0 + jnp.exp(-gate))
    silu = gate * sigma
    hidden = (silu * upper).astype(BF)
    grad_gate = grad_hidden * upper * (sigma * (1.0 + gate * (1.0 - sigma)))
    grads = jnp.concatenate([grad_gate, grad_hidden * silu], axis=1).astype(BF)
    hidden_ref[0, :, :own], grads_ref[0] = hidden, grads
    hidden_ref[0, :, own:] = jnp.zeros((2 * half, hidden_ref.shape[2] - own), BF)
    back = dot(grads, pair_w, 1, 1).astype(BF)
    m_own[0], m_other[0] = back[:half], back[half:]
    out = dot(hidden, down_w, 1, 1).astype(BF)
    y_own[0], y_other[0] = out[:half], out[half:]


def feed(places, weights, rows_two, rows_cot, rows, own):
    (arrays, moves), (cot_arrays, cot_moves) = rows_two, rows_cot
    half, width = rows, arrays[0].shape[1]
    outer = len(weights)
    tokens = 2 * half
    made = [jax.ShapeDtypeStruct((GROUP, half, width), BF)] * 4
    kept = [up_to_lanes(own), 2 * own]
    made += [jax.ShapeDtypeStruct((GROUP, tokens, one), BF) for one in kept]
    return pl.pallas_call(
        functools.partial(feed_kernel, moves, cot_moves, outer),
        grid_spec=pltpu.PrefetchScalarGridSpec(
            num_scalar_prefetch=1,
            grid=(GROUP,),
            in_specs=[ANYWHERE] * (outer + len(arrays) + len(cot_arrays)),
            out_specs=[stepped(half, width)] * 4 + [stepped(tokens, one) for one in kept],
            scratch_shapes=[
                pltpu.VMEM((GROUP, tokens, width), BF),
                pltpu.VMEM((GROUP, tokens, width), BF),
                pltpu.VMEM((outer * GROUP, *weights[0].shape[1:]), BF),
                pltpu.SemaphoreType.DMA((len(arrays),)),
                pltpu.SemaphoreType.DMA((len(cot_arrays),)),
                pltpu.SemaphoreType.DMA((outer,)),
            ],
        ),
        out_shape=made,
        compiler_params=params(),
        cost_estimate=pl.CostEstimate(
            flops=12 * GROUP * tokens * width * own,
            bytes_accessed=8 * GROUP * tokens * width,
            transcendentals=GROUP * tokens * own,
        ),
        name="feed",
    )(places, *weights, *arrays, *cot_arrays)


def grads_kernel(layout, places, *refs):
    count = len(layout)
    pieces, (right, *_, out, held, sems) = refs[:count], refs[count:]
    step = pl.program_id(0)

    @pl.when(step == 0)
    def _():
        copies = moves_of(layout, pieces, held, sems)
        for _, copy in copies:
            copy.start()
        for _, copy in copies:
            copy.wait()

    shards, rows, own = out.shape
    tile = shards * rows
    tokens = held.shape[0] * held.shape[1]
    left = held[:, :, pl.ds(pl.multiple_of(step * tile, 128), tile)].reshape(tokens, tile)
    product = dot(left, right[...].reshape(tokens, own), 0, 0)
    out[...] = product.astype(BF).reshape(shards, rows, own)


def weight_grads(places, pieces, right, shard_rows, columns, at=0, into=None):
    arrays, layout = pieces
    _, tokens, own = right.shape
    width = arrays[0].shape[1]
    tile = 512
    kept = [] if into is None else [into]
    return pl.pallas_call(
        functools.partial(grads_kernel, layout),
        grid_spec=pltpu.PrefetchScalarGridSpec(
            num_scalar_prefetch=1,
            grid=(width // tile,),
            in_specs=[ANYWHERE] * len(arrays) + [whole(right)] + [ANYWHERE] * len(kept),
            out_specs=pl.BlockSpec(
                (tile // shard_rows, shard_rows, own), lambda step, places: (step, 0, at)
            ),
            scratch_shapes=[
                pltpu.VMEM((GROUP, tokens, width), BF),
                pltpu.SemaphoreType.DMA((len(arrays),)),
            ],
        ),
        out_shape=jax.ShapeDtypeStruct((width // shard_rows, shard_rows, columns), BF),
        input_output_aliases={2 + len(arrays): 0} if kept else {},
        compiler_params=params(),
        cost_estimate=pl.CostEstimate(
            flops=2 * GROUP * tokens * width * own,
            bytes_accessed=2 * GROUP * tokens * width,
            transcendentals=0,
        ),
        name="weight_grads",
    )(places, *arrays, right, *kept)


def pack_heads_kernel(qkv, out_weight, gain, note, packed):
    rows, columns = out_weight.shape
    own = columns // GROUP
    for member in range(GROUP):
        for which in range(3):
            first = which * columns + member * own
            part = qkv[:, first : first + own].astype(F32) * gain[...]
            packed[member, :rows, which * own : (which + 1) * own] = part.astype(BF)
        packed[member, :rows, 3 * own :] = out_weight[:, member * own : (member + 1) * own]
        packed[member, rows:, :] = note[...]


def pack_feed_kernel(gate_up, down, gain, packed):
    rows, columns = down.shape
    own = columns // GROUP
    for member in range(GROUP):
        for which in range(2):
            first = which * columns + member * own
            part = (gate_up[:, first : first + own].astype(F32) * gain[...]).astype(BF)
            packed[member, :, which * own : (which + 1) * own] = part
        packed[member, :, 2 * own : 3 * own] = down[:, member * own : (member + 1) * own]
        packed[member, :, 3 * own :] = jnp.zeros((rows, packed.shape[2] - 3 * own), BF)


def gained(gain_ref, sums):
    gain_ref[...] = jnp.broadcast_to(sum(sums), gain_ref.shape)


def unpack_heads_kernel(got, qkv, gain, qkv_ref, out_ref, gain_ref):
    columns = out_ref.shape[1]
    own = columns // GROUP
    sums = []
    for member in range(GROUP):
        total = got[member].astype(F32)
        for which in range(3):
            first = which * columns + member * own
            part = total[:, which * own : (which + 1) * own]
            sums.append(jnp.sum(qkv[:, first : first + own].astype(F32) * part, axis=1, keepdims=True))
            qkv_ref[:, first : first + own] = part * gain[...]
        out_ref[:, member * own : (member + 1) * own] = total[:, 3 * own :]
    gained(gain_ref, sums)


def unpack_feed_kernel(got, got_down, gate_up, gain, gate_up_ref, down_ref, gain_ref):
    columns = down_ref.shape[1]
    own = columns // GROUP
    sums = []
    for member in range(GROUP):
        total = got[member].astype(F32)
        for which in range(2):
            first = which * columns + member * own
            part = total[:, which * own : (which + 1) * own]
            old = gate_up[:, first : first + own].astype(F32)
            sums.append(jnp.sum(old * part, axis=1, keepdims=True))
            gate_up_ref[:, first : first + own] = part * gain[...]
        down_ref[:, member * own : (member + 1) * own] = got_down[member, :, :own].astype(F32)
    gained(gain_ref, sums)


def plain_call(kernel, name, arrays, made):
    in_vmem = pl.BlockSpec(memory_space=pltpu.VMEM)
    return pl.pallas_call(
        kernel,
        in_specs=[in_vmem] * len(arrays),
        out_specs=jax.tree.map(lambda _: in_vmem, made),
        out_shape=made,
        compiler_params=pltpu.CompilerParams(vmem_limit_bytes=VMEM_LIMIT),
        name=name,
    )(*arrays)


def attend_back_kernel(
    moves, shard_rows, outer, places, cosine, sine, mask, q_ref, k_ref, v_ref, *refs
):
    weights, refs = refs[:outer], refs[outer:]
    count = len(moves)
    pieces, refs = refs[:count], refs[count:]
    grad_ref, m_own, m_other, held, weight, sems, weight_sems = refs
    step = pl.program_id(0)
    wait = fetch_weights(weights, weight, weight_sems, step)
    fetch(moves, pieces, held, sems, step)
    wait()
    qkv_w, out_w = head_weights(weight, shard_rows)
    width = out_w.shape[1]
    all_mixed = dot(held[step], out_w, 1, 0).astype(BF)
    made = [[], [], []]
    for low, high in heads_of(width):
        queries, keys, values = (ref[0, :, low:high] for ref in (q_ref, k_ref, v_ref))
        grad_mixed = all_mixed[:, low:high]
        probs = probabilities(queries, keys, mask[0])
        made[2].append(dot(probs.astype(BF), grad_mixed, 0, 0))
        grad_probs = dot(grad_mixed, values, 1, 1)
        delta = jnp.sum(probs * grad_probs, axis=1, keepdims=True)
        grad_scores = (probs * (grad_probs - delta) * (HEAD_DIM**-0.5)).astype(BF)
        made[0].append(turned(dot(grad_scores, keys, 1, 0), cosine[0], -sine[0]))
        made[1].append(turned(dot(grad_scores, queries, 0, 0), cosine[0], -sine[0]))
    grads = jnp.concatenate([part for parts in made for part in parts], axis=1).astype(BF)
    grad_ref[0] = grads
    back = dot(grads, qkv_w, 1, 1).astype(BF)
    half = back.shape[0] // 2
    m_own[0], m_other[0] = back[:half], back[half:]


def attend_back(places, rows_grad, weights, shard_rows, cosine, sine, mask, queries, keys, values):
    arrays, moves = rows_grad
    tokens, width = mask.shape[1], arrays[0].shape[1]
    half = tokens // 2
    outer = len(weights)
    own = weights[0].shape[2] // 4
    made = [jax.ShapeDtypeStruct((GROUP, tokens, 3 * own), BF)]
    made += [jax.ShapeDtypeStruct((GROUP, half, width), BF)] * 2
    return pl.pallas_call(
        functools.partial(attend_back_kernel, moves, shard_rows, outer),
        grid_spec=pltpu.PrefetchScalarGridSpec(
            num_scalar_prefetch=1,
            grid=(GROUP,),
            in_specs=row_specs(tokens)
            + [stepped(tokens, own)] * 3
            + [ANYWHERE] * (outer + len(arrays)),
            out_specs=[stepped(tokens, 3 * own)] + [stepped(half, width)] * 2,
            scratch_shapes=[
                pltpu.VMEM((GROUP, tokens, width), BF),
                pltpu.VMEM((outer * GROUP, *weights[0].shape[1:]), BF),
                pltpu.SemaphoreType.DMA((len(arrays),)),
                pltpu.SemaphoreType.DMA((outer,)),
            ],
        ),
        out_shape=made,
        compiler_params=params(),
        cost_estimate=pl.CostEstimate(
            flops=2 * GROUP * tokens * (width * 4 + 5 * tokens) * own,
            bytes_accessed=4 * GROUP * tokens * width,
            transcendentals=GROUP * tokens * tokens,
        ),
        name="attend_back",
    )(places, cosine, sine, mask, queries, keys, values, *weights, *arrays)


def doc_layout(lengths, positions):
    docs = jnp.arange(lengths.shape[1], dtype=jnp.int32)
    ends_at = jnp.sum(
        jnp.where(docs[None, None, :] <= docs[None, :, None], lengths[:, None, :], 0),
        axis=2,
        dtype=jnp.int32,
    )
    passed = positions[None, :, None] >= ends_at[:, None, :]
    segment = jnp.sum(passed.astype(jnp.int32), axis=2, dtype=jnp.int32)
    doc_start = jnp.sum(jnp.where(passed, lengths[:, None, :], 0), axis=2, dtype=jnp.int32)
    offset = (positions[None, :] - doc_start).astype(F32)
    allowed = (segment[:, :, None] == segment[:, None, :]) & (
        positions[None, :, None] >= positions[None, None, :]
    )
    half_dim = HEAD_DIM // 2
    inverse = jnp.exp(
        jnp.arange(half_dim, dtype=F32) * (-2.0 * math.log(10000.0) / HEAD_DIM)
    )
    angles = offset[:, :, None] * inverse
    cosine, sine = jnp.cos(angles), jnp.sin(angles)
    return (
        allowed.astype(BF),
        jnp.concatenate([cosine, cosine], axis=2),
        jnp.concatenate([-sine, sine], axis=2),
    )


def rms_scale(values):
    return lax.rsqrt(jnp.mean(values * values, axis=-1, keepdims=True) + EPS_NORM)


def norm_back(grad_normed, normed, scale):
    return scale * (
        grad_normed - normed * jnp.mean(grad_normed * normed, axis=-1, keepdims=True)
    )


def shards(
    tokens,
    norm1_gain,
    qkv_weight,
    out_weight,
    norm2_gain,
    gate_up_weight,
    down_weight,
    doc_lengths,
    cotangent,
):
    rows, width = tokens.shape
    place = lax.axis_index("dp")
    core = lax.axis_index("tensor")
    member = place % GROUP
    outer = lax.axis_size("dp") // GROUP
    row_count = 2 * rows
    shard_rows, _, local_width = qkv_weight.shape
    own_width = local_width // GROUP
    own_hidden = gate_up_weight.shape[2] // GROUP
    places = jnp.arange(GROUP, dtype=jnp.int32) ^ member
    order = ring()
    spot = sum(jnp.where(place // GROUP == one, i, 0) for i, one in enumerate(order))
    back = [order[-i % outer] for i in range(outer)]

    def turn(shaped, by):
        twice = jnp.concatenate([shaped, shaped], axis=1)
        return lax.dynamic_slice_in_dim(twice, by, outer, axis=1)

    def rolled(x):
        shaped = x.reshape(rows, outer, width // outer)
        shaped = jnp.stack([shaped[:, one] for one in back], axis=1)
        return turn(shaped, (outer - spot) % outer).reshape(x.shape)

    def unrolled(x):
        shaped = turn(x.reshape(rows, outer, width // outer), spot)
        return jnp.stack([shaped[:, back.index(one)] for one in range(outer)], axis=1).reshape(x.shape)

    gain_one = norm1_gain.astype(F32)[:, None]
    gain_two = norm2_gain.astype(F32)[:, None]

    residual = rolled(tokens).astype(F32)
    scale_one = rms_scale(residual)
    normed_one = residual * scale_one
    blocks_one = gather(normed_one.astype(BF))
    rows_one = part_of(with_other_core(blocks_one), 0, rows)
    qkv_flat = qkv_weight.reshape(shard_rows, 3 * local_width)
    docs = doc_lengths.shape[1]
    note = jnp.pad(doc_lengths.astype(BF), ((0, 15), (0, 4 * own_width - docs)))
    head_own = swap_members(
        plain_call(
            pack_heads_kernel,
            "pack_heads",
            [qkv_flat, out_weight, gain_one, note],
            jax.ShapeDtypeStruct((GROUP, shard_rows + 16, 4 * own_width), BF),
        )
    )
    head_mats = outer_gather(head_own)
    chosen = (jnp.arange(GROUP, dtype=jnp.int32)[None, :] == places[:, None])[:, :, None]
    lengths = jnp.sum(
        jnp.where(chosen, head_own[:, shard_rows, :docs].astype(F32)[None], 0.0), axis=1
    ).astype(jnp.int32)
    positions = (jnp.arange(row_count, dtype=jnp.int32) + rows * core) % row_count
    mask, cosine, sine = doc_layout(lengths, positions)

    gate_up_flat = gate_up_weight.reshape(shard_rows, 2 * GROUP * own_hidden)
    feed_packed = plain_call(
        pack_feed_kernel,
        "pack_feed",
        [gate_up_flat, down_weight, gain_two],
        jax.ShapeDtypeStruct((GROUP, shard_rows, up_to_lanes(3 * own_hidden)), BF),
    )
    feed_own = swap_members(after(feed_packed, blocks_one[1]))
    feed_mats = outer_gather(feed_own)
    cot_own = rolled(cotangent)
    blocks_cot = gather(after(cot_own, blocks_one[3]))
    rows_cot = part_of(with_other_core(blocks_cot), 0, rows)

    a_own, a_other, mixed, queries, keys, values = attend(
        places, rows_one, head_mats, shard_rows, cosine, sine, after(mask, feed_own)
    )
    attn_blocks = after_all(both_cores(a_own, a_other), *blocks_cot[1:3])
    attn = reduce_last(*reduce_first(attn_blocks))
    stream = residual + attn
    scale_two = rms_scale(stream)
    normed_two = stream * scale_two
    blocks_two = gather(after(normed_two.astype(BF), blocks_cot[3], feed_mats[1]))
    rows_two = part_of(with_other_core(blocks_two), 0, rows)

    m_own, m_other, y_own, y_other, hidden, grads = feed(
        places, feed_mats, rows_two, rows_cot, rows, own_hidden
    )
    down_part = weight_grads(places, rows_cot, hidden, shard_rows, hidden.shape[2])
    down_got, down_sum = outer_reduce(down_part)
    terms = reduce_first(after_all(both_cores(m_own, m_other), down_part))
    pair_part = weight_grads(places, rows_two, grads, shard_rows, grads.shape[2])
    pair_got, pair_sum = outer_reduce(pair_part)
    back_two = reduce_last(*after_all(terms, pair_part, down_got[0]))
    grad_stream = cot_own.astype(F32) + norm_back(back_two, normed_two, scale_two)

    grad_low = after(grad_stream.astype(BF), pair_got[0])
    blocks_grad = gather(grad_low)
    rows_grad = part_of(with_other_core(blocks_grad), 0, rows)
    y_terms = reduce_first(after_all(both_cores(y_own, y_other), blocks_grad[1]))
    grad_qkv, m_own, m_other = attend_back(
        places,
        rows_grad,
        head_mats,
        shard_rows,
        cosine,
        sine,
        after(mask, down_got[1]),
        queries,
        keys,
        values,
    )
    head_part = weight_grads(places, rows_grad, mixed, shard_rows, 4 * own_width, 3)
    head_part = weight_grads(
        places, rows_one, grad_qkv, shard_rows, 4 * own_width, 0, head_part
    )
    _, head_sum = outer_reduce(head_part)
    terms = reduce_first(after_all(both_cores(m_own, m_other), head_part, pair_got[1]))
    down_got, pair_got = swap_members(down_sum), swap_members(pair_sum)
    head_got = swap_members(head_sum)
    mlp_out = reduce_last(*after_all(y_terms, terms[1]))
    gate_up_grad, down_grad, gain_two_part = plain_call(
        unpack_feed_kernel,
        "unpack_feed",
        [pair_got, down_got, gate_up_flat, gain_two],
        [
            jax.ShapeDtypeStruct(gate_up_flat.shape, F32),
            jax.ShapeDtypeStruct(down_weight.shape, F32),
            jax.ShapeDtypeStruct((shard_rows, 128), F32),
        ],
    )
    back_one = reduce_last(*terms)

    output = unrolled((stream + mlp_out).astype(BF))
    input_grad = unrolled((grad_stream + norm_back(back_one, normed_one, scale_one)).astype(BF))
    qkv_grad, out_grad, gain_one_part = plain_call(
        unpack_heads_kernel,
        "unpack_heads",
        [head_got, qkv_flat, gain_one],
        [
            jax.ShapeDtypeStruct(qkv_flat.shape, F32),
            jax.ShapeDtypeStruct(out_weight.shape, F32),
            jax.ShapeDtypeStruct((shard_rows, 128), F32),
        ],
    )
    gain_two_part, gain_one_part = gain_two_part[:, 0], gain_one_part[:, 0]
    return (
        output,
        input_grad,
        gain_one_part + over_cores(gain_one_part),
        qkv_grad.reshape(qkv_weight.shape),
        out_grad,
        gain_two_part + over_cores(gain_two_part),
        gate_up_grad.reshape(gate_up_weight.shape),
        down_grad,
    )


def solution(mesh):
    placed = (
        P(("dp", "tensor"), None),
        P("dp"),
        P("dp", None, "tensor"),
        P("dp", "tensor"),
        P("dp"),
        P("dp", None, "tensor"),
        P("dp", "tensor"),
        P("dp", None),
        P(("dp", "tensor"), None),
    )
    return jax.shard_map(
        shards,
        mesh=mesh,
        in_specs=placed,
        out_specs=(
            P(("dp", "tensor"), None),
            P(("dp", "tensor"), None),
            P("dp"),
            P("dp", None, "tensor"),
            P("dp", "tensor"),
            P("dp"),
            P("dp", None, "tensor"),
            P("dp", "tensor"),
        ),
        check_vma=False,
    )
```

profile of v0, /device:TPU:24, one launch (start us, length us, event | category | flops | bytes accessed | tf_op | source)
XLA Modules:
  0.0 580.5 jit_solution(7329738235544068669)
XLA Ops:
  13.2 15.0 %all-to-all-done.refs_0_ = bf16[4,144,1024]{2,1,0:T(8,128)(2,1)} async-done(((bf16[4,144,1024]{2,1,0:T(8,128)(2,1)}), bf16[4,144,1024]{2,1,0:T(8,128)(2,1)}, u32[]{:S(2)}, u32[]{:S(2)}) %all-to-all-start) | async-done | bytes 1179680 | tf_op jit(solution)/shard_map/all_to_all | solution.py:90
  35.6 20.7 %collective-permute-done.1.refs_1_ = bf16[4,144,1024]{2,1,0:T(8,128)(2,1)} collective-permute-done((bf16[4,144,1024]{2,1,0:T(8,128)(2,1)}, bf16[4,144,1024]{2,1,0:T(8,128)(2,1)}, u32[]{:S(2)}, u32[]{:S(2)}) %collective-permute-start.1) | collective-permute-done | bytes 1179680 | tf_op jit(solution)/shard_map/ppermute | solution.py:43
  70.1 13.4 %collective-permute-done.2.refs_2_ = bf16[4,144,1024]{2,1,0:T(8,128)(2,1)} collective-permute-done((bf16[4,144,1024]{2,1,0:T(8,128)(2,1)}, bf16[4,144,1024]{2,1,0:T(8,128)(2,1)}, u32[]{:S(2)}, u32[]{:S(2)}) %collective-permute-start.2) | collective-permute-done | bytes 1179680 | tf_op jit(solution)/shard_map/ppermute | solution.py:43
  83.8 18.8 %collective-permute-done.8.refs_10_.refs_6_ = bf16[128,2048]{1,0:T(8,128)(2,1)S(1)} collective-permute-done((bf16[128,2048]{1,0:T(8,128)(2,1)}, bf16[128,2048]{1,0:T(8,128)(2,1)S(1)}, u32[]{:S(2)}, u32[]{:S(2)}) %collective-permute-start.8) | collective-permute-done | bytes 524320 | tf_op jit(solution)/shard_map/ppermute | solution.py:23
  109.9 15.9 %attend.1 = (bf16[4,128,2048]{2,1,0:T(8,128)(2,1)}, bf16[4,128,2048]{2,1,0:T(8,128)(2,1)}, bf16[4,256,256]{2,1,0:T(8,128)(2,1)}, bf16[4,256,256]{2,1,0:T(8,128)(...) custom-call(s32[4]{0:T(128)} %copy-done.29, f32[4,256,128]{2,1,0:T(8,128)} %pad_maximum_fusion.cosine, ...), custom_call_target="tpu_custom_call" | custom-call | flops 4563402752 | bytes 8388608 | tf_op jit(solution)/shard_map/attend/pallas_call | solution.py:250
  126.2 32.4 %collective-permute-done.16.refs_1_ = bf16[4,128,2176]{2,1,0:T(8,128)(2,1)} collective-permute-done((bf16[4,128,2176]{2,1,0:T(8,128)(2,1)}, bf16[4,128,2176]{2,1,0:T(8,128)(2,1)}, u32[]{:S(2)}, u32[]{:S(2)}) %collective-permute-start.16) | collective-permute-done | bytes 2228256 | tf_op jit(solution)/shard_map/ppermute | solution.py:43
  167.0 9.2 %collective-permute-done.12.refs_16_.refs_4_ = bf16[128,2048]{1,0:T(8,128)(2,1)S(1)} collective-permute-done((bf16[128,2048]{1,0:T(8,128)(2,1)S(1)}, bf16[128,2048]{1,0:T(8,128)(2,1)S(1)}, u32[]{:S(2)}, u32[]{:S(2)}) %collective-permute-start.12) | collective-permute-done | bytes 524320 | tf_op jit(solution)/shard_map/ppermute | solution.py:23
  178.3 12.8 %collective-permute-done.13 = bf16[128,2048]{1,0:T(8,128)(2,1)S(1)} collective-permute-done((bf16[128,2048]{1,0:T(8,128)(2,1)S(1)}, bf16[128,2048]{1,0:T(8,128)(2,1)S(1)}, u32[]{:S(2)}, u32[]{:S(2)}) %collective-permute-start.13) | collective-permute-done | bytes 524320 | tf_op jit(solution)/shard_map/ppermute | solution.py:23
  193.5 16.8 %collective-permute-done.17.refs_2_ = bf16[4,128,2176]{2,1,0:T(8,128)(2,1)} collective-permute-done((bf16[4,128,2176]{2,1,0:T(8,128)(2,1)}, bf16[4,128,2176]{2,1,0:T(8,128)(2,1)}, u32[]{:S(2)}, u32[]{:S(2)}) %collective-permute-start.17) | collective-permute-done | bytes 2228256 | tf_op jit(solution)/shard_map/ppermute | solution.py:43
  211.3 11.8 %collective-permute-done.19.refs_18_.refs_6_ = bf16[128,2048]{1,0:T(8,128)(2,1)S(1)} collective-permute-done((bf16[128,2048]{1,0:T(8,128)(2,1)S(1)}, bf16[128,2048]{1,0:T(8,128)(2,1)S(1)}, u32[]{:S(2)}, u32[]{:S(2)}) %collective-permute-start.19) | collective-permute-done | bytes 524320 | tf_op jit(solution)/shard_map/ppermute | solution.py:23
  225.3 9.6 %collective-permute-done.21.refs_6_.refs_2_ = bf16[128,2048]{1,0:T(8,128)(2,1)S(1)} collective-permute-done((bf16[128,2048]{1,0:T(8,128)(2,1)S(1)}, bf16[128,2048]{1,0:T(8,128)(2,1)S(1)}, u32[]{:S(2)}, u32[]{:S(2)}) %collective-permute-start.21) | collective-permute-done | bytes 524320 | tf_op jit(solution)/shard_map/ppermute | solution.py:23
  239.8 10.3 %collective-permute-done.25.refs_10_.refs_6_ = bf16[128,2048]{1,0:T(8,128)(2,1)S(1)} collective-permute-done((bf16[128,2048]{1,0:T(8,128)(2,1)S(1)}, bf16[128,2048]{1,0:T(8,128)(2,1)S(1)}, u32[]{:S(2)}, u32[]{:S(2)}) %collective-permute-start.25) | collective-permute-done | bytes 524320 | tf_op jit(solution)/shard_map/ppermute | solution.py:23
  250.2 10.6 %collective-permute-done.18.refs_3_ = bf16[4,128,2176]{2,1,0:T(8,128)(2,1)} collective-permute-done((bf16[4,128,2176]{2,1,0:T(8,128)(2,1)}, bf16[4,128,2176]{2,1,0:T(8,128)(2,1)}, u32[]{:S(2)}, u32[]{:S(2)}) %collective-permute-start.18) | collective-permute-done | bytes 2228256 | tf_op jit(solution)/shard_map/ppermute | solution.py:43
  260.9 29.0 %feed.1 = (bf16[4,128,2048]{2,1,0:T(8,128)(2,1)}, bf16[4,128,2048]{2,1,0:T(8,128)(2,1)}, bf16[4,128,2048]{2,1,0:T(8,128)(2,1)}, bf16[4,128,2048]{2,1,0:T(8,128)(...) custom-call(s32[4]{0:T(128)} %copy-done.29, bf16[4,128,2176]{2,1,0:T(8,128)(2,1)} %all-to-all-done.1.refs_0_, ...), custom_call_target="tpu_custom_call" | custom-call | flops 17716740096 | bytes 16777216 | tf_op jit(solution)/shard_map/feed/pallas_call | solution.py:316
  290.0 13.3 %weight_grads.5 = bf16[16,128,1408]{2,1,0:T(8,128)(2,1)} custom-call(s32[4]{0:T(128)} %copy-done.29, bf16[128,2048]{1,0:T(8,128)(2,1)} %copy-done.28, bf16[128,2048]{1,0:T(8,128)(2,1)} %copy-done.40, bf16[128,2048]{1,0:T(8,128)(2,1)} %copy-done.37, bf16[128,2048]{1,0:T(8,128)(2,1)} %copy-done.42, bf16[128,2048]{1,0:T(8,128)(2,1)} %copy-done.38, ...), custom_call_target="tpu_custom_call" | custom-call | flops 5905580032 | bytes 4194304 | tf_op jit(solution)/shard_map/weight_grads/pallas_call | solution.py:370
  306.1 9.6 %weight_grads.4 = bf16[16,128,768]{2,1,0:T(8,128)(2,1)} custom-call(s32[4]{0:T(128)} %copy-done.29, bf16[128,2048]{1,0:T(8,128)(2,1)} %bitcast.64, bf16[128,2048]{1,0:T(8,128)(2,1)} %copy-done.32, bf16[128,2048]{1,0:T(8,128)(2,1)} %copy-done.31, bf16[128,2048]{1,0:T(8,128)(2,1)} %copy-done.35, bf16[128,2048]{1,0:T(8,128)(2,1)} %copy-done.30, ...), custom_call_target="tpu_custom_call" | custom-call | flops 3221225472 | bytes 4194304 | tf_op jit(solution)/shard_map/weight_grads/pallas_call | solution.py:370
  322.0 11.2 %collective-permute-done.33 = bf16[128,2048]{1,0:T(8,128)(2,1)S(1)} collective-permute-done((bf16[128,2048]{1,0:T(8,128)(2,1)S(1)}, bf16[128,2048]{1,0:T(8,128)(2,1)S(1)}, u32[]{:S(2)}, u32[]{:S(2)}) %collective-permute-start.33) | collective-permute-done | bytes 524320 | tf_op jit(solution)/shard_map/ppermute | solution.py:23
  333.3 24.7 %collective-permute-done.34 = bf16[4,128,768]{2,1,0:T(8,128)(2,1)S(1)} collective-permute-done((bf16[4,128,768]{2,1,0:T(8,128)(2,1)S(1)}, bf16[4,128,768]{2,1,0:T(8,128)(2,1)S(1)}, u32[]{:S(2)}, u32[]{:S(2)}) %collective-permute-start.34) | collective-permute-done | bytes 786464 | tf_op jit(solution)/shard_map/ppermute | solution.py:43
  362.9 8.6 %collective-permute-done.35 = bf16[128,2048]{1,0:T(8,128)(2,1)S(1)} collective-permute-done((bf16[128,2048]{1,0:T(8,128)(2,1)S(1)}, bf16[128,2048]{1,0:T(8,128)(2,1)S(1)}, u32[]{:S(2)}, u32[]{:S(2)}) %collective-permute-start.35) | collective-permute-done | bytes 524320 | tf_op jit(solution)/shard_map/ppermute | solution.py:23
  377.2 10.0 %collective-permute-done.38.refs_6_.refs_2_ = bf16[128,2048]{1,0:T(8,128)(2,1)S(1)} collective-permute-done((bf16[128,2048]{1,0:T(8,128)(2,1)S(1)}, bf16[128,2048]{1,0:T(8,128)(2,1)S(1)}, u32[]{:S(2)}, u32[]{:S(2)}) %collective-permute-start.38) | collective-permute-done | bytes 524320 | tf_op jit(solution)/shard_map/ppermute | solution.py:23
  388.6 24.7 %collective-permute-done.40 = bf16[4,128,768]{2,1,0:T(8,128)(2,1)S(1)} collective-permute-done((bf16[4,128,768]{2,1,0:T(8,128)(2,1)S(1)}, bf16[4,128,768]{2,1,0:T(8,128)(2,1)S(1)}, u32[]{:S(2)}, u32[]{:S(2)}) %collective-permute-start.40) | collective-permute-done | bytes 786464 | tf_op jit(solution)/shard_map/ppermute | solution.py:43
  419.0 18.7 %attend_back.1 = (bf16[4,256,768]{2,1,0:T(8,128)(2,1)}, bf16[4,128,2048]{2,1,0:T(8,128)(2,1)}, bf16[4,128,2048]{2,1,0:T(8,128)(2,1)}) custom-call(s32[4]{0:T(128)} %copy-done.29, f32[4,256,128]{2,1,0:T(8,128)} %pad_maximum_fusion.cosine, f32[4,256,128]{2,1,0:T(8,128)} %pad_maximum_fusion.1.sine, bf16[4,256,256]{2,1,0:T(8,128)(2,1)} %and_convert_fusion.mask, ...), custom_call_target="tpu_custom_call" | custom-call | flops 4966055936 | bytes 8388608 | tf_op jit(solution)/shard_map/attend_back/pallas_call | solution.py:507
  448.4 9.7 %weight_grads.7 = bf16[16,128,1024]{2,1,0:T(8,128)(2,1)} custom-call(s32[4]{0:T(128)} %copy-done.29, bf16[128,2048]{1,0:T(8,128)(2,1)} %copy-done.12, bf16[128,2048]{1,0:T(8,128)(2,1)} %collective-permute-done.4.refs_5_.refs_1_, bf16[128,2048]{1,0:T(8,128)(2,1)} %collective-permute-done.refs_6_.refs_2_, ...), custom_call_target="tpu_custom_call", output_to_operand_aliasing={{}: (10, {})} | custom-call | flops 3221225472 | bytes 4194304 | tf_op jit(solution)/shard_map/weight_grads/pallas_call | solution.py:370
  460.6 9.0 %collective-permute-done.59 = bf16[4,128,768]{2,1,0:T(8,128)(2,1)S(1)} collective-permute-done((bf16[4,128,768]{2,1,0:T(8,128)(2,1)}, bf16[4,128,768]{2,1,0:T(8,128)(2,1)S(1)}, u32[]{:S(2)}, u32[]{:S(2)}) %collective-permute-start.59) | collective-permute-done | bytes 786464 | tf_op jit(solution)/shard_map/ppermute | solution.py:43
  (295 shorter events, 212.6 us)
Async XLA Ops:
  33.6 35.2 %collective-permute-start.6 = (bf16[128,2048]{1,0:T(8,128)(2,1)S(1)}, bf16[128,2048]{1,0:T(8,128)(2,1)}, u32[]{:S(2)}, u32[]{:S(2)}) collective-permute-start(bf16[128,2048]{1,0:T(8,128)(2,1)S(1)} %multiply_convert_fusion.1.refs_4_.refs_0_), channel_id=1, source_target_pairs={{0,4},{2,6},{4,0},{6,2},{8,12},{10,14},{12,8},{14,10},{16,20},{18,... | collective-permute-start | bytes 1572872 | tf_op jit(solution)/shard_map/ppermute | solution.py:23
  35.1 71.4 %collective-permute-start.4 = (bf16[128,2048]{1,0:T(8,128)(2,1)S(1)}, bf16[128,2048]{1,0:T(8,128)(2,1)}, u32[]{:S(2)}, u32[]{:S(2)}) collective-permute-start(bf16[128,2048]{1,0:T(8,128)(2,1)S(1)} %multiply_convert_fusion.1.refs_4_.refs_0_), channel_id=1, source_target_pairs={{0,1},{1,0},{2,3},{3,2},{4,5},{5,4},{6,7},{7,6},{8,9},{9,8},{10,11... | collective-permute-start | bytes 1572872 | tf_op jit(solution)/shard_map/ppermute | solution.py:27
  62.2 44.4 %all-to-all-start.1 = ((bf16[4,128,2176]{2,1,0:T(8,128)(2,1)}), bf16[4,128,2176]{2,1,0:T(8,128)(2,1)}, u32[]{:S(2)}, u32[]{:S(2)}) async-start(bf16[4,128,2176]{2,1,0:T(8,128)(2,1)} %pack_feed.1), calls=%async_computation.1 | async-start | bytes 4456448 | tf_op jit(solution)/shard_map/all_to_all | solution.py:90
  66.8 35.9 %collective-permute-start.8 = (bf16[128,2048]{1,0:T(8,128)(2,1)}, bf16[128,2048]{1,0:T(8,128)(2,1)S(1)}, u32[]{:S(2)}, u32[]{:S(2)}) collective-permute-start(bf16[128,2048]{1,0:T(8,128)(2,1)} %collective-permute-done.refs_6_.refs_2_), channel_id=1, source_target_pairs={{0,4},{2,6},{4,0},{6,2},{8,12},{10,14},{12,8},{14,10},{16,20},{18,... | collective-permute-start | bytes 1572872 | tf_op jit(solution)/shard_map/ppermute | solution.py:23
  68.8 39.5 %collective-permute-start.5 = (bf16[128,2048]{1,0:T(8,128)(2,1)}, bf16[128,2048]{1,0:T(8,128)(2,1)}, u32[]{:S(2)}, u32[]{:S(2)}) collective-permute-start(bf16[128,2048]{1,0:T(8,128)(2,1)} %collective-permute-done.refs_6_.refs_2_), channel_id=1, source_target_pairs={{0,1},{1,0},{2,3},{3,2},{4,5},{5,4},{6,7},{7,6},{8,9},{9,8},{10,11... | collective-permute-start | bytes 1572872 | tf_op jit(solution)/shard_map/ppermute | solution.py:27
  68.8 39.5 %collective-permute-start.7 = (bf16[128,2048]{1,0:T(8,128)(2,1)}, bf16[128,2048]{1,0:T(8,128)(2,1)}, u32[]{:S(2)}, u32[]{:S(2)}) collective-permute-start(bf16[128,2048]{1,0:T(8,128)(2,1)} %collective-permute-done.6.refs_8_.refs_4_), channel_id=1, source_target_pairs={{0,1},{1,0},{2,3},{3,2},{4,5},{5,4},{6,7},{7,6},{8,9},{9,8},{10,11... | collective-permute-start | bytes 1572872 | tf_op jit(solution)/shard_map/ppermute | solution.py:27
  106.6 52.1 %collective-permute-start.16 = (bf16[4,128,2176]{2,1,0:T(8,128)(2,1)}, bf16[4,128,2176]{2,1,0:T(8,128)(2,1)}, u32[]{:S(2)}, u32[]{:S(2)}) collective-permute-start(bf16[4,128,2176]{2,1,0:T(8,128)(2,1)} %all-to-all-done.1.refs_0_), channel_id=1, source_target_pairs={{0,8},{2,10},{4,12},{6,14},{8,24},{10,26},{12,28},{14,30},{24,16},... | collective-permute-start | bytes 6684680 | tf_op jit(solution)/shard_map/ppermute | solution.py:43
  125.8 38.9 %collective-permute-start.10 = (bf16[4,128,2048]{2,1,0:T(8,128)(2,1)}, bf16[4,128,2048]{2,1,0:T(8,128)(2,1)}, u32[]{:S(2)}, u32[]{:S(2)}) collective-permute-start(bf16[4,128,2048]{2,1,0:T(8,128)(2,1)} %get-tuple-element.60), channel_id=1, source_target_pairs={{0,1},{1,0},{2,3},{3,2},{4,5},{5,4},{6,7},{7,6},{8,9},{9,8},{10,11... | collective-permute-start | bytes 6291464 | tf_op jit(solution)/shard_map/ppermute | solution.py:27
  158.6 51.7 %collective-permute-start.17 = (bf16[4,128,2176]{2,1,0:T(8,128)(2,1)}, bf16[4,128,2176]{2,1,0:T(8,128)(2,1)}, u32[]{:S(2)}, u32[]{:S(2)}) collective-permute-start(bf16[4,128,2176]{2,1,0:T(8,128)(2,1)} %collective-permute-done.16.refs_1_), channel_id=1, source_target_pairs={{0,8},{2,10},{4,12},{6,14},{8,24},{10,26},{12,28},{14,30},{24,16},... | collective-permute-start | bytes 6684680 | tf_op jit(solution)/shard_map/ppermute | solution.py:43
  178.0 32.7 %collective-permute-start.15 = (bf16[128,2048]{1,0:T(8,128)(2,1)S(1)}, bf16[128,2048]{1,0:T(8,128)(2,1)S(1)}, u32[]{:S(2)}, u32[]{:S(2)}) collective-permute-start(bf16[128,2048]{1,0:T(8,128)(2,1)S(1)} %get-tuple-element.65), channel_id=1, source_target_pairs={{0,4},{2,6},{4,0},{6,2},{8,12},{10,14},{12,8},{14,10},{16,20},{18,... | collective-permute-start | bytes 1572872 | tf_op jit(solution)/shard_map/ppermute | solution.py:23
  193.0 31.5 %collective-permute-start.27 = (bf16[128,2048]{1,0:T(8,128)(2,1)S(1)}, bf16[128,2048]{1,0:T(8,128)(2,1)S(1)}, u32[]{:S(2)}, u32[]{:S(2)}) collective-permute-start(bf16[128,2048]{1,0:T(8,128)(2,1)S(1)} %bitcast.62), channel_id=1, source_target_pairs={{0,1},{1,0},{2,3},{3,2},{4,5},{5,4},{6,7},{7,6},{8,9},{9,8},{10,11... | collective-permute-start | bytes 1572872 | tf_op jit(solution)/shard_map/ppermute | solution.py:27
  193.0 32.1 %collective-permute-start.29 = (bf16[128,2048]{1,0:T(8,128)(2,1)S(1)}, bf16[128,2048]{1,0:T(8,128)(2,1)S(1)}, u32[]{:S(2)}, u32[]{:S(2)}) collective-permute-start(bf16[128,2048]{1,0:T(8,128)(2,1)S(1)} %collective-permute-done.12.refs_16_.refs_4_), channel_id=1, source_target_pairs={{0,1},{1,0},{2,3},{3,2},{4,5},{5,4},{6,7},{7,6},{8,9},{9,8},{10,11... | collective-permute-start | bytes 1572872 | tf_op jit(solution)/shard_map/ppermute | solution.py:27
  210.7 50.1 %collective-permute-start.18 = (bf16[4,128,2176]{2,1,0:T(8,128)(2,1)}, bf16[4,128,2176]{2,1,0:T(8,128)(2,1)}, u32[]{:S(2)}, u32[]{:S(2)}) collective-permute-start(bf16[4,128,2176]{2,1,0:T(8,128)(2,1)} %collective-permute-done.17.refs_2_), channel_id=1, source_target_pairs={{0,8},{2,10},{4,12},{6,14},{8,24},{10,26},{12,28},{14,30},{24,16},... | collective-permute-start | bytes 6684680 | tf_op jit(solution)/shard_map/ppermute | solution.py:43
  305.9 55.3 %collective-permute-start.37 = (bf16[4,128,1408]{2,1,0:T(8,128)(2,1)}, bf16[4,128,1408]{2,1,0:T(8,128)(2,1)S(1)}, u32[]{:S(2)}, u32[]{:S(2)}) collective-permute-start(bf16[4,128,1408]{2,1,0:T(8,128)(2,1)} %slice.278), channel_id=1, source_target_pairs={{0,8},{2,10},{4,12},{6,14},{8,24},{10,26},{12,28},{14,30},{24,16},... | collective-permute-start | bytes 4325384 | tf_op jit(solution)/shard_map/ppermute | solution.py:43
  320.6 37.4 %collective-permute-start.34 = (bf16[4,128,768]{2,1,0:T(8,128)(2,1)S(1)}, bf16[4,128,768]{2,1,0:T(8,128)(2,1)S(1)}, u32[]{:S(2)}, u32[]{:S(2)}) collective-permute-start(bf16[4,128,768]{2,1,0:T(8,128)(2,1)S(1)} %slice.277), channel_id=1, source_target_pairs={{0,8},{2,10},{4,12},{6,14},{8,24},{10,26},{12,28},{14,30},{24,16},... | collective-permute-start | bytes 2359304 | tf_op jit(solution)/shard_map/ppermute | solution.py:43
  362.9 51.5 %collective-permute-start.48 = (bf16[4,128,1408]{2,1,0:T(8,128)(2,1)S(1)}, bf16[4,128,1408]{2,1,0:T(8,128)(2,1)S(1)}, u32[]{:S(2)}, u32[]{:S(2)}) collective-permute-start(bf16[4,128,1408]{2,1,0:T(8,128)(2,1)S(1)} %add_convert_fusion.2), channel_id=1, source_target_pairs={{0,8},{2,10},{4,12},{6,14},{8,24},{10,26},{12,28},{14,30},{24,16},... | collective-permute-start | bytes 4325384 | tf_op jit(solution)/shard_map/ppermute | solution.py:43
  375.4 38.0 %collective-permute-start.40 = (bf16[4,128,768]{2,1,0:T(8,128)(2,1)S(1)}, bf16[4,128,768]{2,1,0:T(8,128)(2,1)S(1)}, u32[]{:S(2)}, u32[]{:S(2)}) collective-permute-start(bf16[4,128,768]{2,1,0:T(8,128)(2,1)S(1)} %add_convert_fusion.8), channel_id=1, source_target_pairs={{0,8},{2,10},{4,12},{6,14},{8,24},{10,26},{12,28},{14,30},{24,16},... | collective-permute-start | bytes 2359304 | tf_op jit(solution)/shard_map/ppermute | solution.py:43
  375.4 38.4 %collective-permute-start.43 = (bf16[128,2048]{1,0:T(8,128)(2,1)S(1)}, bf16[128,2048]{1,0:T(8,128)(2,1)S(1)}, u32[]{:S(2)}, u32[]{:S(2)}) collective-permute-start(bf16[128,2048]{1,0:T(8,128)(2,1)S(1)} %get-tuple-element.80.refs_4_.refs_0_), channel_id=1, source_target_pairs={{0,4},{2,6},{4,0},{6,2},{8,12},{10,14},{12,8},{14,10},{16,20},{18,... | collective-permute-start | bytes 1572872 | tf_op jit(solution)/shard_map/ppermute | solution.py:23
  417.2 58.2 %collective-permute-start.58 = (bf16[4,128,1408]{2,1,0:T(8,128)(2,1)}, bf16[4,128,1408]{2,1,0:T(8,128)(2,1)}, u32[]{:S(2)}, u32[]{:S(2)}) collective-permute-start(bf16[4,128,1408]{2,1,0:T(8,128)(2,1)} %add_convert_fusion.1), channel_id=1, source_target_pairs={{0,8},{2,10},{4,12},{6,14},{8,24},{10,26},{12,28},{14,30},{24,16},... | collective-permute-start | bytes 4325384 | tf_op jit(solution)/shard_map/ppermute | solution.py:43
  437.7 57.0 %collective-permute-start.47 = (bf16[4,128,2048]{2,1,0:T(8,128)(2,1)}, bf16[4,128,2048]{2,1,0:T(8,128)(2,1)}, u32[]{:S(2)}, u32[]{:S(2)}) collective-permute-start(bf16[4,128,2048]{2,1,0:T(8,128)(2,1)} %get-tuple-element.90), channel_id=1, source_target_pairs={{0,1},{1,0},{2,3},{3,2},{4,5},{5,4},{6,7},{7,6},{8,9},{9,8},{10,11... | collective-permute-start | bytes 6291464 | tf_op jit(solution)/shard_map/ppermute | solution.py:27
  440.1 29.5 %collective-permute-start.59 = (bf16[4,128,768]{2,1,0:T(8,128)(2,1)}, bf16[4,128,768]{2,1,0:T(8,128)(2,1)S(1)}, u32[]{:S(2)}, u32[]{:S(2)}) collective-permute-start(bf16[4,128,768]{2,1,0:T(8,128)(2,1)} %add_convert_fusion.7), channel_id=1, source_target_pairs={{0,8},{2,10},{4,12},{6,14},{8,24},{10,26},{12,28},{14,30},{24,16},... | collective-permute-start | bytes 2359304 | tf_op jit(solution)/shard_map/ppermute | solution.py:43
  441.2 57.7 %collective-permute-start.31 = (bf16[4,128,2048]{2,1,0:T(8,128)(2,1)}, bf16[4,128,2048]{2,1,0:T(8,128)(2,1)}, u32[]{:S(2)}, u32[]{:S(2)}) collective-permute-start(bf16[4,128,2048]{2,1,0:T(8,128)(2,1)} %get-tuple-element.68), channel_id=1, source_target_pairs={{0,1},{1,0},{2,3},{3,2},{4,5},{5,4},{6,7},{7,6},{8,9},{9,8},{10,11... | collective-permute-start | bytes 6291464 | tf_op jit(solution)/shard_map/ppermute | solution.py:27
  460.3 31.1 %collective-permute-start.54 = (bf16[4,128,1024]{2,1,0:T(8,128)(2,1)}, bf16[4,128,1024]{2,1,0:T(8,128)(2,1)}, u32[]{:S(2)}, u32[]{:S(2)}) collective-permute-start(bf16[4,128,1024]{2,1,0:T(8,128)(2,1)} %slice.291), channel_id=1, source_target_pairs={{0,8},{2,10},{4,12},{6,14},{8,24},{10,26},{12,28},{14,30},{24,16},... | collective-permute-start | bytes 3145736 | tf_op jit(solution)/shard_map/ppermute | solution.py:43
  502.3 28.4 %collective-permute-start.39 = (bf16[128,2048]{1,0:T(8,128)(2,1)}, bf16[128,2048]{1,0:T(8,128)(2,1)}, u32[]{:S(2)}, u32[]{:S(2)}) collective-permute-start(bf16[128,2048]{1,0:T(8,128)(2,1)} %get-tuple-element.83), channel_id=1, source_target_pairs={{0,4},{2,6},{4,0},{6,2},{8,12},{10,14},{12,8},{14,10},{16,20},{18,... | collective-permute-start | bytes 1572872 | tf_op jit(solution)/shard_map/ppermute | solution.py:23
  (86 other events, 1313.0 us)
where the time goes:
time: 592 us; the launch traced here: 580 us
  waiting for transfers between devices  307 us (52%)
  Pallas kernels  119 us (20%)
  other arithmetic  59.6 us (10%)
  starting transfers between devices  54.7 us (9%)
  local copies, waits for them, and re-layouts  38.3 us (6%)
    ppermute x15, waiting for transfers between devices, over_ring(): lax.ppermute(x, 'dp', [(GROUP * a + i, GROUP * b + i) for a, b in pairs f...  161 us
    ppermute x24, waiting for transfers between devices, over_dp(): return lax.ppermute(x, 'dp', [(i, i ^ bit) for i in range(size)])  117 us
    pallas_call x4, Pallas kernels, weight_grads(): pl.pallas_call(functools.partial(grads_kernel, layout), grid_spec=pltpu.P...  39.6 us
    convert_element_type x17, other arithmetic, plus(): return (base.astype(F32) + more.astype(F32)).astype(BF)  37.6 us
    all_to_all x5, waiting for transfers between devices, swap_members(): lax.all_to_all(blocks, 'dp', split_axis=0, concat_axis=0, tiled=True, axi...  29.1 us
    pallas_call x1, Pallas kernels, feed(): pl.pallas_call(functools.partial(feed_kernel, moves, cot_moves, outer), g...  29 us
    ppermute x24, starting transfers between devices, over_dp(): return lax.ppermute(x, 'dp', [(i, i ^ bit) for i in range(size)])  26.7 us
    all_to_all x5, starting transfers between devices, swap_members(): lax.all_to_all(blocks, 'dp', split_axis=0, concat_axis=0, tiled=True, axi...  19.6 us
  transfers between devices with their start and end apart: 66, of which 31 were waited for; matrix products, arithmetic and copies ran while one was open for 15% of the time, Pallas kernels for 14%

commit v1 on v0

--- a/solution.py
+++ b/solution.py
@@ -99,12 +99,12 @@
     return blocks
 
 
-def outer_reduce(part):
-    chunks = part.reshape(-1, GROUP, *part.shape[1:])
-    got = [over_ring(chunks[1])]
-    for k in range(2, chunks.shape[0]):
-        got.append(over_ring(plus(got[-1], chunks[k])))
-    return got, plus(got[-1], chunks[0])
+def outer_reduce(first, others, waits=()):
+    got, sums = [over_ring(first)], []
+    for i, chunk in enumerate(others[:-1]):
+        sums.append(plus(got[-1], chunk))
+        got.append(over_ring(after(sums[-1], waits[i]) if i < len(waits) else sums[-1]))
+    return got, [*sums, plus(got[-1], others[-1])]
 
 
 def dot(left, right, left_dim, right_dim):
@@ -276,8 +276,8 @@
     weights, refs = refs[:outer], refs[outer:]
     count, cot_count = len(moves), len(cot_moves)
     pieces, cots, refs = refs[:count], refs[count : count + cot_count], refs[count + cot_count :]
-    m_own, m_other, y_own, y_other, hidden_ref, grads_ref, *refs = refs
-    held, held_cot, weight, sems, cot_sems, weight_sems = refs
+    m_own, m_other, hidden_ref, grads_ref, first_ref, *refs = refs
+    held, held_cot, hidden_held, grads_held, weight, sems, cot_sems, weight_sems = refs
     step = pl.program_id(0)
     wait = fetch_weights(weights, weight, weight_sems, step)
     fetch(moves, pieces, held, sems, step)
@@ -297,12 +297,30 @@
     hidden = (silu * upper).astype(BF)
     grad_gate = grad_hidden * upper * (sigma * (1.0 + gate * (1.0 - sigma)))
     grads = jnp.concatenate([grad_gate, grad_hidden * silu], axis=1).astype(BF)
-    hidden_ref[0, :, :own], grads_ref[0] = hidden, grads
-    hidden_ref[0, :, own:] = jnp.zeros((2 * half, hidden_ref.shape[2] - own), BF)
+    hidden_held[step, :, :own] = hidden
+    hidden_held[step, :, own:] = jnp.zeros((2 * half, hidden_ref.shape[2] - own), BF)
+    grads_held[step] = grads
+    hidden_ref[0], grads_ref[0] = hidden_held[step], grads
     back = dot(grads, pair_w, 1, 1).astype(BF)
     m_own[0], m_other[0] = back[:half], back[half:]
-    out = dot(hidden, down_w, 1, 1).astype(BF)
-    y_own[0], y_other[0] = out[:half], out[half:]
+
+    @pl.when(step == GROUP - 1)
+    def _():
+        members, shard_rows, _ = first_ref.shape
+        wide, tokens = members * shard_rows, GROUP * 2 * half
+        column = 0
+        for left, right in ((held, grads_held), (held_cot, hidden_held)):
+            columns = right.shape[2]
+            product = dot(
+                left[:, :, wide : 2 * wide].reshape(tokens, wide),
+                right[...].reshape(tokens, columns),
+                0,
+                0,
+            )
+            first_ref[:, :, column : column + columns] = product.astype(BF).reshape(
+                members, shard_rows, columns
+            )
+            column += columns
 
 
 def feed(places, weights, rows_two, rows_cot, rows, own):
@@ -310,19 +328,25 @@
     half, width = rows, arrays[0].shape[1]
     outer = len(weights)
     tokens = 2 * half
-    made = [jax.ShapeDtypeStruct((GROUP, half, width), BF)] * 4
     kept = [up_to_lanes(own), 2 * own]
+    first = (GROUP, weights[0].shape[1], sum(kept))
+    made = [jax.ShapeDtypeStruct((GROUP, half, width), BF)] * 2
     made += [jax.ShapeDtypeStruct((GROUP, tokens, one), BF) for one in kept]
+    made += [jax.ShapeDtypeStruct(first, BF)]
     return pl.pallas_call(
         functools.partial(feed_kernel, moves, cot_moves, outer),
         grid_spec=pltpu.PrefetchScalarGridSpec(
             num_scalar_prefetch=1,
             grid=(GROUP,),
             in_specs=[ANYWHERE] * (outer + len(arrays) + len(cot_arrays)),
-            out_specs=[stepped(half, width)] * 4 + [stepped(tokens, one) for one in kept],
+            out_specs=[stepped(half, width)] * 2
+            + [stepped(tokens, one) for one in kept]
+            + [pl.BlockSpec(first, lambda step, places: (0, 0, 0))],
             scratch_shapes=[
                 pltpu.VMEM((GROUP, tokens, width), BF),
                 pltpu.VMEM((GROUP, tokens, width), BF),
+                pltpu.VMEM((GROUP, tokens, kept[0]), BF),
+                pltpu.VMEM((GROUP, tokens, kept[1]), BF),
                 pltpu.VMEM((outer * GROUP, *weights[0].shape[1:]), BF),
                 pltpu.SemaphoreType.DMA((len(arrays),)),
                 pltpu.SemaphoreType.DMA((len(cot_arrays),)),
@@ -332,80 +356,127 @@
         out_shape=made,
         compiler_params=params(),
         cost_estimate=pl.CostEstimate(
-            flops=12 * GROUP * tokens * width * own,
-            bytes_accessed=8 * GROUP * tokens * width,
+            flops=10 * GROUP * tokens * width * own,
+            bytes_accessed=6 * GROUP * tokens * width,
             transcendentals=GROUP * tokens * own,
         ),
         name="feed",
     )(places, *weights, *arrays, *cot_arrays)
 
 
-def grads_kernel(layout, places, *refs):
-    count = len(layout)
-    pieces, (right, *_, out, held, sems) = refs[:count], refs[count:]
+def feed_out_kernel(first, outer, places, hidden, *refs):
+    weights, (y_own, y_other, weight, sems) = refs[:outer], refs[outer:]
     step = pl.program_id(0)
-
-    @pl.when(step == 0)
-    def _():
-        copies = moves_of(layout, pieces, held, sems)
-        for _, copy in copies:
-            copy.start()
-        for _, copy in copies:
-            copy.wait()
-
-    shards, rows, own = out.shape
-    tile = shards * rows
-    tokens = held.shape[0] * held.shape[1]
-    left = held[:, :, pl.ds(pl.multiple_of(step * tile, 128), tile)].reshape(tokens, tile)
-    product = dot(left, right[...].reshape(tokens, own), 0, 0)
-    out[...] = product.astype(BF).reshape(shards, rows, own)
-
-
-def weight_grads(places, pieces, right, shard_rows, columns, at=0, into=None):
-    arrays, layout = pieces
-    _, tokens, own = right.shape
-    width = arrays[0].shape[1]
-    tile = 512
-    kept = [] if into is None else [into]
+    own = weight.shape[2]
+    parts = [ref.at[:, :, pl.ds(first, own)] for ref in weights]
+    fetch_weights(parts, weight, sems, step)()
+    down_w = weight[...].reshape(y_own.shape[2], own)
+    out = dot(hidden[0], down_w, 1, 1).astype(BF)
+    half = out.shape[0] // 2
+    y_own[0], y_other[0] = out[:half], out[half:]
+
+
+def feed_out(places, weights, hidden, rows, width, own):
+    outer, tokens = len(weights), 2 * rows
+    columns = hidden.shape[2]
     return pl.pallas_call(
-        functools.partial(grads_kernel, layout),
+        functools.partial(feed_out_kernel, 2 * own, outer),
         grid_spec=pltpu.PrefetchScalarGridSpec(
             num_scalar_prefetch=1,
-            grid=(width // tile,),
-            in_specs=[ANYWHERE] * len(arrays) + [whole(right)] + [ANYWHERE] * len(kept),
-            out_specs=pl.BlockSpec(
-                (tile // shard_rows, shard_rows, own), lambda step, places: (step, 0, at)
-            ),
+            grid=(GROUP,),
+            in_specs=[stepped(tokens, columns)] + [ANYWHERE] * outer,
+            out_specs=[stepped(rows, width)] * 2,
             scratch_shapes=[
-                pltpu.VMEM((GROUP, tokens, width), BF),
-                pltpu.SemaphoreType.DMA((len(arrays),)),
+                pltpu.VMEM((outer * GROUP, weights[0].shape[1], columns), BF),
+                pltpu.SemaphoreType.DMA((outer,)),
             ],
         ),
-        out_shape=jax.ShapeDtypeStruct((width // shard_rows, shard_rows, columns), BF),
-        input_output_aliases={2 + len(arrays): 0} if kept else {},
+        out_shape=[jax.ShapeDtypeStruct((GROUP, rows, width), BF)] * 2,
         compiler_params=params(),
         cost_estimate=pl.CostEstimate(
             flops=2 * GROUP * tokens * width * own,
-            bytes_accessed=2 * GROUP * tokens * width,
+            bytes_accessed=4 * GROUP * tokens * width,
             transcendentals=0,
         ),
+        name="feed_out",
+    )(places, hidden, *weights)
+
+
+def grads_kernel(all_moves, chunks, count_outs, *refs):
+    counts = [1 + max(move[0] for move in moves) for moves in all_moves]
+    lefts = []
+    for count in counts:
+        lefts.append(refs[:count])
+        refs = refs[count:]
+    rights, refs = refs[: len(lefts)], refs[len(lefts) :]
+    outs, (held, sems) = refs[: len(chunks) * count_outs], refs[len(chunks) * count_outs :]
+    wide = held.shape[4]
+    waits = []
+    for i, chunk in enumerate(chunks):
+        for part, (pieces, moves) in enumerate(zip(lefts, all_moves)):
+            for index, source, step, row, rows in moves:
+                copy = pltpu.make_async_copy(
+                    pieces[index].at[pl.ds(source, rows), pl.ds(chunk * wide, wide)],
+                    held.at[i, part, step, pl.ds(row, rows)],
+                    sems.at[i, part, index],
+                )
+                copy.start()
+                waits.append((i, copy))
+    for i in range(len(chunks)):
+        for at, copy in waits:
+            if at == i:
+                copy.wait()
+        products = []
+        for part, right in enumerate(rights):
+            tokens, own = right.shape[0] * right.shape[1], right.shape[2]
+            product = dot(held[i, part].reshape(tokens, wide), right[...].reshape(tokens, own), 0, 0)
+            products.append(product.astype(BF))
+        product = products[0] if len(products) == 1 else jnp.concatenate(products, axis=1)
+        column = 0
+        for out in outs[i * count_outs : (i + 1) * count_outs]:
+            members, rows, own = out.shape
+            out[...] = product[:, column : column + own].reshape(members, rows, own)
+            column += own
+
+
+def weight_grads(lefts, rights, shard_rows, chunks, widths):
+    tokens = rights[0].shape[1]
+    wide = GROUP * shard_rows
+    in_vmem = pl.BlockSpec(memory_space=pltpu.VMEM)
+    pieces = [array for arrays, _ in lefts for array in arrays]
+    made = [jax.ShapeDtypeStruct((GROUP, shard_rows, width), BF) for width in widths]
+    results = pl.pallas_call(
+        functools.partial(grads_kernel, [moves for _, moves in lefts], chunks, len(widths)),
+        in_specs=[ANYWHERE] * len(pieces) + [in_vmem] * len(rights),
+        out_specs=[in_vmem] * (len(made) * len(chunks)),
+        scratch_shapes=[
+            pltpu.VMEM((len(chunks), len(lefts), GROUP, tokens, wide), BF),
+            pltpu.SemaphoreType.DMA((len(chunks), len(lefts), len(lefts[0][0]))),
+        ],
+        out_shape=made * len(chunks),
+        compiler_params=pltpu.CompilerParams(vmem_limit_bytes=VMEM_LIMIT),
+        cost_estimate=pl.CostEstimate(
+            flops=2 * GROUP * tokens * wide * len(chunks) * sum(r.shape[2] for r in rights),
+            bytes_accessed=2 * GROUP * tokens * wide * len(chunks),
+            transcendentals=0,
+        ),
         name="weight_grads",
-    )(places, *arrays, right, *kept)
-
-
-def pack_heads_kernel(qkv, out_weight, gain, note, packed):
-    rows, columns = out_weight.shape
+    )(*pieces, *rights)
+    return [results[i : i + len(made)] for i in range(0, len(results), len(made))]
+
+
+def pack_heads_kernel(qkv, out_weight, gain, packed):
+    columns = out_weight.shape[1]
     own = columns // GROUP
     for member in range(GROUP):
         for which in range(3):
             first = which * columns + member * own
             part = qkv[:, first : first + own].astype(F32) * gain[...]
-            packed[member, :rows, which * own : (which + 1) * own] = part.astype(BF)
-        packed[member, :rows, 3 * own :] = out_weight[:, member * own : (member + 1) * own]
-        packed[member, rows:, :] = note[...]
-
-
-def pack_feed_kernel(gate_up, down, gain, packed):
+            packed[member, :, which * own : (which + 1) * own] = part.astype(BF)
+        packed[member, :, 3 * own :] = out_weight[:, member * own : (member + 1) * own]
+
+
+def pack_feed_kernel(gate_up, down, gain, lengths, packed):
     rows, columns = down.shape
     own = columns // GROUP
     for member in range(GROUP):
@@ -414,19 +485,21 @@
             part = (gate_up[:, first : first + own].astype(F32) * gain[...]).astype(BF)
             packed[member, :, which * own : (which + 1) * own] = part
         packed[member, :, 2 * own : 3 * own] = down[:, member * own : (member + 1) * own]
-        packed[member, :, 3 * own :] = jnp.zeros((rows, packed.shape[2] - 3 * own), BF)
+        packed[member, :, 3 * own :] = jnp.broadcast_to(
+            lengths[:, : packed.shape[2] - 3 * own], (rows, packed.shape[2] - 3 * own)
+        )
 
 
 def gained(gain_ref, sums):
     gain_ref[...] = jnp.broadcast_to(sum(sums), gain_ref.shape)
 
 
-def unpack_heads_kernel(got, qkv, gain, qkv_ref, out_ref, gain_ref):
+def unpack_heads_kernel(got, got_more, qkv, gain, qkv_ref, out_ref, gain_ref):
     columns = out_ref.shape[1]
     own = columns // GROUP
     sums = []
     for member in range(GROUP):
-        total = got[member].astype(F32)
+        total = jnp.concatenate([got[member], got_more[member]], axis=1).astype(F32)
         for which in range(3):
             first = which * columns + member * own
             part = total[:, which * own : (which + 1) * own]
@@ -436,7 +509,7 @@
     gained(gain_ref, sums)
 
 
-def unpack_feed_kernel(got, got_down, gate_up, gain, gate_up_ref, down_ref, gain_ref):
+def unpack_feed_kernel(got, gate_up, gain, gate_up_ref, down_ref, gain_ref):
     columns = down_ref.shape[1]
     own = columns // GROUP
     sums = []
@@ -448,7 +521,7 @@
             old = gate_up[:, first : first + own].astype(F32)
             sums.append(jnp.sum(old * part, axis=1, keepdims=True))
             gate_up_ref[:, first : first + own] = part * gain[...]
-        down_ref[:, member * own : (member + 1) * own] = got_down[member, :, :own].astype(F32)
+        down_ref[:, member * own : (member + 1) * own] = total[:, 2 * own : 3 * own]
     gained(gain_ref, sums)
 
 
@@ -612,35 +685,38 @@
     residual = rolled(tokens).astype(F32)
     scale_one = rms_scale(residual)
     normed_one = residual * scale_one
-    blocks_one = gather(normed_one.astype(BF))
+    qkv_flat = qkv_weight.reshape(shard_rows, 3 * local_width)
+    head_packed = plain_call(
+        pack_heads_kernel,
+        "pack_heads",
+        [qkv_flat, out_weight, gain_one],
+        jax.ShapeDtypeStruct((GROUP, shard_rows, 4 * own_width), BF),
+    )
+    head_own = swap_members(head_packed)
+    blocks_one = gather(after(normed_one.astype(BF), head_packed))
     rows_one = part_of(with_other_core(blocks_one), 0, rows)
-    qkv_flat = qkv_weight.reshape(shard_rows, 3 * local_width)
+    head_mats = outer_gather(head_own)
+    gate_up_flat = gate_up_weight.reshape(shard_rows, 2 * GROUP * own_hidden)
+    spare = up_to_lanes(3 * own_hidden) - 3 * own_hidden
     docs = doc_lengths.shape[1]
-    note = jnp.pad(doc_lengths.astype(BF), ((0, 15), (0, 4 * own_width - docs)))
-    head_own = swap_members(
-        plain_call(
-            pack_heads_kernel,
-            "pack_heads",
-            [qkv_flat, out_weight, gain_one, note],
-            jax.ShapeDtypeStruct((GROUP, shard_rows + 16, 4 * own_width), BF),
-        )
-    )
-    head_mats = outer_gather(head_own)
-    chosen = (jnp.arange(GROUP, dtype=jnp.int32)[None, :] == places[:, None])[:, :, None]
-    lengths = jnp.sum(
-        jnp.where(chosen, head_own[:, shard_rows, :docs].astype(F32)[None], 0.0), axis=1
-    ).astype(jnp.int32)
-    positions = (jnp.arange(row_count, dtype=jnp.int32) + rows * core) % row_count
-    mask, cosine, sine = doc_layout(lengths, positions)
-
-    gate_up_flat = gate_up_weight.reshape(shard_rows, 2 * GROUP * own_hidden)
+    assert docs <= spare
     feed_packed = plain_call(
         pack_feed_kernel,
         "pack_feed",
-        [gate_up_flat, down_weight, gain_two],
-        jax.ShapeDtypeStruct((GROUP, shard_rows, up_to_lanes(3 * own_hidden)), BF),
-    )
-    feed_own = swap_members(after(feed_packed, blocks_one[1]))
+        [
+            gate_up_flat,
+            down_weight,
+            gain_two,
+            jnp.pad(doc_lengths.astype(BF), ((0, 0), (0, 128 - docs))),
+        ],
+        jax.ShapeDtypeStruct((GROUP, shard_rows, 3 * own_hidden + spare), BF),
+    )
+    feed_own = swap_members(after(feed_packed, blocks_one[3]))
+    notes = feed_own[:, 0, 3 * own_hidden : 3 * own_hidden + docs].astype(F32)
+    chosen = (jnp.arange(GROUP, dtype=jnp.int32)[None, :] == places[:, None])[:, :, None]
+    lengths = jnp.sum(jnp.where(chosen, notes[None], 0.0), axis=1).astype(jnp.int32)
+    positions = (jnp.arange(row_count, dtype=jnp.int32) + rows * core) % row_count
+    mask, cosine, sine = doc_layout(lengths, positions)
     feed_mats = outer_gather(feed_own)
     cot_own = rolled(cotangent)
     blocks_cot = gather(after(cot_own, blocks_one[3]))
@@ -657,19 +733,22 @@
     blocks_two = gather(after(normed_two.astype(BF), blocks_cot[3], feed_mats[1]))
     rows_two = part_of(with_other_core(blocks_two), 0, rows)
 
-    m_own, m_other, y_own, y_other, hidden, grads = feed(
+    m_own, m_other, hidden, grads, feed_first = feed(
         places, feed_mats, rows_two, rows_cot, rows, own_hidden
     )
-    down_part = weight_grads(places, rows_cot, hidden, shard_rows, hidden.shape[2])
-    down_got, down_sum = outer_reduce(down_part)
-    terms = reduce_first(after_all(both_cores(m_own, m_other), down_part))
-    pair_part = weight_grads(places, rows_two, grads, shard_rows, grads.shape[2])
-    pair_got, pair_sum = outer_reduce(pair_part)
-    back_two = reduce_last(*after_all(terms, pair_part, down_got[0]))
+    ones, rest = [1], [*range(2, outer), 0]
+    feed_args = [rows_two, rows_cot], [grads, hidden], shard_rows
+    widths = [grads.shape[2] + hidden.shape[2]]
+    terms = reduce_first(both_cores(m_own, m_other))
+    feed_rest = [one for [one] in weight_grads(*feed_args, rest, widths)]
+    y_own, y_other = feed_out(
+        places, feed_mats, after(hidden, terms[1]), rows, width, own_hidden
+    )
+    back_two = reduce_last(*after_all(terms, feed_rest[0]))
+    feed_got, feed_sums = outer_reduce(feed_first, feed_rest)
     grad_stream = cot_own.astype(F32) + norm_back(back_two, normed_two, scale_two)
 
-    grad_low = after(grad_stream.astype(BF), pair_got[0])
-    blocks_grad = gather(grad_low)
+    blocks_grad = gather(after(grad_stream.astype(BF), feed_sums[0]))
     rows_grad = part_of(with_other_core(blocks_grad), 0, rows)
     y_terms = reduce_first(after_all(both_cores(y_own, y_other), blocks_grad[1]))
     grad_qkv, m_own, m_other = attend_back(
@@ -679,38 +758,44 @@
         shard_rows,
         cosine,
         sine,
-        after(mask, down_got[1]),
+        after(mask, y_terms[1], feed_sums[1]),
         queries,
         keys,
         values,
     )
-    head_part = weight_grads(places, rows_grad, mixed, shard_rows, 4 * own_width, 3)
-    head_part = weight_grads(
-        places, rows_one, grad_qkv, shard_rows, 4 * own_width, 0, head_part
-    )
-    _, head_sum = outer_reduce(head_part)
-    terms = reduce_first(after_all(both_cores(m_own, m_other), head_part, pair_got[1]))
-    down_got, pair_got = swap_members(down_sum), swap_members(pair_sum)
-    head_got = swap_members(head_sum)
+    head_args = [rows_one, rows_grad], [grad_qkv, mixed], shard_rows
+    widths = [2 * own_width] * 2
+    [head_first] = weight_grads(*head_args, ones, widths)
+    head_args = head_args[0], [after(grad_qkv, *head_first), mixed], shard_rows
+    head_rest = weight_grads(*head_args, rest, widths)
+    terms = reduce_first(after_all(both_cores(m_own, m_other), *head_first))
+    back_one = reduce_last(*terms)
     mlp_out = reduce_last(*after_all(y_terms, terms[1]))
+    head_first = after_all(head_first, feed_got[-1])
+    head_sums = [
+        outer_reduce(one, [chunk[i] for chunk in head_rest], (terms[1], back_one))[1][-1] for i, one in enumerate(head_first)
+    ]
+    feed_back = swap_members(after(feed_sums[-1], back_one))
     gate_up_grad, down_grad, gain_two_part = plain_call(
         unpack_feed_kernel,
         "unpack_feed",
-        [pair_got, down_got, gate_up_flat, gain_two],
+        [feed_back, gate_up_flat, gain_two],
         [
             jax.ShapeDtypeStruct(gate_up_flat.shape, F32),
             jax.ShapeDtypeStruct(down_weight.shape, F32),
             jax.ShapeDtypeStruct((shard_rows, 128), F32),
         ],
     )
-    back_one = reduce_last(*terms)
 
     output = unrolled((stream + mlp_out).astype(BF))
     input_grad = unrolled((grad_stream + norm_back(back_one, normed_one, scale_one)).astype(BF))
+    gate_up_grad = gate_up_grad.reshape(gate_up_weight.shape)
+    head_got = [swap_members(after(one, feed_back)) for one in head_sums[:1]]
+    head_got.append(swap_members(after(head_sums[1], gate_up_grad)))
     qkv_grad, out_grad, gain_one_part = plain_call(
         unpack_heads_kernel,
         "unpack_heads",
-        [head_got, qkv_flat, gain_one],
+        [*head_got, qkv_flat, gain_one],
         [
             jax.ShapeDtypeStruct(qkv_flat.shape, F32),
             jax.ShapeDtypeStruct(out_weight.shape, F32),
@@ -725,7 +810,7 @@
         qkv_grad.reshape(qkv_weight.shape),
         out_grad,
         gain_two_part + over_cores(gain_two_part),
-        gate_up_grad.reshape(gate_up_weight.shape),
+        gate_up_grad,
         down_grad,
     )
 

time: 592 us -> 579 us (0.978)
  other arithmetic: 59.6 us -> 51.1 us
    all_to_all x5, waiting for transfers between devices: 29.1 us -> 12.4 us  [swap_members(): lax.all_to_all(blocks, 'dp', split_axis=0, concat_axis=0, tiled=True, axi...]
    ppermute x24, waiting for transfers between devices: 117 us -> 130 us  [over_dp(): return lax.ppermute(x, 'dp', [(i, i ^ bit) for i in range(size)])]
    convert_element_type x17 -> x16, other arithmetic: 37.6 us -> 31.1 us  [plus(): return (base.astype(F32) + more.astype(F32)).astype(BF)]
  transfers between devices with their start and end apart: 66 -> 66, of which waited for: 31 -> 29; matrix products, arithmetic and copies ran while one was open for 15% -> 12% of each run, Pallas kernels for 14% -> 15%
where the time goes in v1:
time: 579 us; the launch traced here: 568 us
  waiting for transfers between devices  310 us (54%)
  Pallas kernels  118 us (20%)
  starting transfers between devices  53.3 us (9%)
  other arithmetic  51.1 us (9%)
  local copies, waits for them, and re-layouts  32.8 us (6%)
    ppermute x15, waiting for transfers between devices, over_ring(): lax.ppermute(x, 'dp', [(GROUP * a + i, GROUP * b + i) for a, b in pairs f...  163 us
    ppermute x24, waiting for transfers between devices, over_dp(): return lax.ppermute(x, 'dp', [(i, i ^ bit) for i in range(size)])  130 us
    pallas_call x1, Pallas kernels, feed(): pl.pallas_call(functools.partial(feed_kernel, moves, cot_moves, outer), g...  31.3 us
    convert_element_type x16, other arithmetic, plus(): return (base.astype(F32) + more.astype(F32)).astype(BF)  31.1 us
    pallas_call x3, Pallas kernels, weight_grads(): pl.pallas_call(functools.partial(grads_kernel, [moves for _, moves in lef...  27.8 us
    ppermute x24, starting transfers between devices, over_dp(): return lax.ppermute(x, 'dp', [(i, i ^ bit) for i in range(size)])  21.6 us
    all_to_all x5, starting transfers between devices, swap_members(): lax.all_to_all(blocks, 'dp', split_axis=0, concat_axis=0, tiled=True, axi...  20.8 us
    pallas_call x1, Pallas kernels, attend_back(): pl.pallas_call(functools.partial(attend_back_kernel, moves, shard_rows, o...  18.5 us
  transfers between devices with their start and end apart: 66, of which 29 were waited for; matrix products, arithmetic and copies ran while one was open for 12% of the time, Pallas kernels for 15%

profile of v1, /device:TPU:24, one launch (start us, length us, event | category | flops | bytes accessed | tf_op | source)
XLA Modules:
  0.0 567.9 jit_solution(9169084921842327127)
XLA Ops:
  17.8 9.1 %collective-permute-done.refs_6_.refs_2_ = bf16[128,2048]{1,0:T(8,128)(2,1)S(1)} collective-permute-done((bf16[128,2048]{1,0:T(8,128)(2,1)S(1)}, bf16[128,2048]{1,0:T(8,128)(2,1)S(1)}, u32[]{:S(2)}, u32[]{:S(2)}) %collective-permute-start) | collective-permute-done | bytes 524320 | tf_op jit(solution)/shard_map/ppermute | solution.py:23
  50.2 12.1 %collective-permute-done.2.refs_1_ = bf16[4,128,1024]{2,1,0:T(8,128)(2,1)} collective-permute-done((bf16[4,128,1024]{2,1,0:T(8,128)(2,1)}, bf16[4,128,1024]{2,1,0:T(8,128)(2,1)}, u32[]{:S(2)}, u32[]{:S(2)}) %collective-permute-start.2) | collective-permute-done | bytes 1048608 | tf_op jit(solution)/shard_map/ppermute | solution.py:43
  62.6 22.9 %collective-permute-done.7.refs_8_.refs_4_ = bf16[128,2048]{1,0:T(8,128)(2,1)S(1)} collective-permute-done((bf16[128,2048]{1,0:T(8,128)(2,1)S(1)}, bf16[128,2048]{1,0:T(8,128)(2,1)S(1)}, u32[]{:S(2)}, u32[]{:S(2)}) %collective-permute-start.7) | collective-permute-done | bytes 524320 | tf_op jit(solution)/shard_map/ppermute | solution.py:23
  93.6 20.8 %collective-permute-done.4.refs_3_ = bf16[4,128,1024]{2,1,0:T(8,128)(2,1)} collective-permute-done((bf16[4,128,1024]{2,1,0:T(8,128)(2,1)}, bf16[4,128,1024]{2,1,0:T(8,128)(2,1)}, u32[]{:S(2)}, u32[]{:S(2)}) %collective-permute-start.4) | collective-permute-done | bytes 1048608 | tf_op jit(solution)/shard_map/ppermute | solution.py:43
  114.4 15.7 %attend.1 = (bf16[4,128,2048]{2,1,0:T(8,128)(2,1)}, bf16[4,128,2048]{2,1,0:T(8,128)(2,1)}, bf16[4,256,256]{2,1,0:T(8,128)(2,1)}, bf16[4,256,256]{2,1,0:T(8,128)(...) custom-call(s32[4]{0:T(128)} %copy-done.51, f32[4,256,128]{2,1,0:T(8,128)} %pad_maximum_fusion.cosine, ...), custom_call_target="tpu_custom_call" | custom-call | flops 4563402752 | bytes 8388608 | tf_op jit(solution)/shard_map/attend/pallas_call | solution.py:250
  137.6 23.5 %collective-permute-done.16.refs_1_ = bf16[4,128,2176]{2,1,0:T(8,128)(2,1)} collective-permute-done((bf16[4,128,2176]{2,1,0:T(8,128)(2,1)}, bf16[4,128,2176]{2,1,0:T(8,128)(2,1)}, u32[]{:S(2)}, u32[]{:S(2)}) %collective-permute-start.16) | collective-permute-done | bytes 2228256 | tf_op jit(solution)/shard_map/ppermute | solution.py:43
  165.6 12.8 %collective-permute-done.13 = bf16[128,2048]{1,0:T(8,128)(2,1)S(1)} collective-permute-done((bf16[128,2048]{1,0:T(8,128)(2,1)S(1)}, bf16[128,2048]{1,0:T(8,128)(2,1)S(1)}, u32[]{:S(2)}, u32[]{:S(2)}) %collective-permute-start.13) | collective-permute-done | bytes 524320 | tf_op jit(solution)/shard_map/ppermute | solution.py:23
  180.7 9.0 %collective-permute-done.15 = bf16[128,2048]{1,0:T(8,128)(2,1)S(1)} collective-permute-done((bf16[128,2048]{1,0:T(8,128)(2,1)S(1)}, bf16[128,2048]{1,0:T(8,128)(2,1)S(1)}, u32[]{:S(2)}, u32[]{:S(2)}) %collective-permute-start.15) | collective-permute-done | bytes 524320 | tf_op jit(solution)/shard_map/ppermute | solution.py:23
  190.1 21.6 %collective-permute-done.17.refs_2_ = bf16[4,128,2176]{2,1,0:T(8,128)(2,1)S(1)} collective-permute-done((bf16[4,128,2176]{2,1,0:T(8,128)(2,1)}, bf16[4,128,2176]{2,1,0:T(8,128)(2,1)S(1)}, u32[]{:S(2)}, u32[]{:S(2)}) %collective-permute-start.17) | collective-permute-done | bytes 2228256 | tf_op jit(solution)/shard_map/ppermute | solution.py:43
  214.3 9.9 %collective-permute-done.21.refs_6_.refs_2_ = bf16[128,2048]{1,0:T(8,128)(2,1)S(1)} collective-permute-done((bf16[128,2048]{1,0:T(8,128)(2,1)S(1)}, bf16[128,2048]{1,0:T(8,128)(2,1)S(1)}, u32[]{:S(2)}, u32[]{:S(2)}) %collective-permute-start.21) | collective-permute-done | bytes 524320 | tf_op jit(solution)/shard_map/ppermute | solution.py:23
  228.5 10.4 %collective-permute-done.25.refs_10_.refs_6_ = bf16[128,2048]{1,0:T(8,128)(2,1)S(1)} collective-permute-done((bf16[128,2048]{1,0:T(8,128)(2,1)S(1)}, bf16[128,2048]{1,0:T(8,128)(2,1)S(1)}, u32[]{:S(2)}, u32[]{:S(2)}) %collective-permute-start.25) | collective-permute-done | bytes 524320 | tf_op jit(solution)/shard_map/ppermute | solution.py:23
  241.6 19.9 %collective-permute-done.18.refs_3_ = bf16[4,128,2176]{2,1,0:T(8,128)(2,1)} collective-permute-done((bf16[4,128,2176]{2,1,0:T(8,128)(2,1)S(1)}, bf16[4,128,2176]{2,1,0:T(8,128)(2,1)}, u32[]{:S(2)}, u32[]{:S(2)}) %collective-permute-start.18) | collective-permute-done | bytes 2228256 | tf_op jit(solution)/shard_map/ppermute | solution.py:43
  261.5 31.3 %feed.1 = (bf16[4,128,2048]{2,1,0:T(8,128)(2,1)}, bf16[4,128,2048]{2,1,0:T(8,128)(2,1)}, bf16[4,256,768]{2,1,0:T(8,128)(2,1)}, bf16[4,256,1408]{2,1,0:T(8,128)(2,1)}, bf16[4,128,2176]{2,1,0:T(8,128)(2,1)}) custom-call(s32[4]{0:T(128)} %copy-done.51, bf16[4,128,2176]{2,1,0:T(8,128)(2,1)} %all-to-all-done.refs_0_, ...), custom_call_target="tpu_custom_call" | custom-call | flops 14763950080 | bytes 12582912 | tf_op jit(solution)/shard_map/feed/pallas_call | solution.py:336
  300.8 14.2 %weight_grads.3 = (bf16[4,128,2176]{2,1,0:T(8,128)(2,1)}, bf16[4,128,2176]{2,1,0:T(8,128)(2,1)}, bf16[4,128,2176]{2,1,0:T(8,128)(2,1)}) custom-call(bf16[128,2048]{1,0:T(8,128)(2,1)} %copy-done.30, bf16[128,2048]{1,0:T(8,128)(2,1)} %copy-done.44, bf16[128,2048]{1,0:T(8,128)(2,1)} %copy-done.38, bf16[128,2048]{1,0:T(8,128)(2,1)} %copy-done.45, ...), custom_call_target="tpu_custom_call" | custom-call | flops 6845104128 | bytes 3145728 | tf_op jit(solution)/shard_map/weight_grads/pallas_call | solution.py:448
  319.7 8.9 %feed_out.1 = (bf16[4,128,2048]{2,1,0:T(8,128)(2,1)}, bf16[4,128,2048]{2,1,0:T(8,128)(2,1)}) custom-call(s32[4]{0:T(128)} %copy-done.51, bf16[4,256,768]{2,1,0:T(8,128)(2,1)} %get-tuple-element.91.hidden.refs_17_, bf16[4,128,2176]{2,1,0:T(8,128)(2,1)} %all-to-all-done.refs_0_, bf16[4,128,2176]{2,1,0:T(8,128)(2,1)} %collective-permute-done.16.refs_1_, ...), custom_call_target="tpu_custom_call" | custom-call | flops 2952790016 | bytes 8388608 | tf_op jit(solution)/shard_map/feed_out/pallas_call | solution.py:382
  328.7 16.7 %collective-permute-done.36 = bf16[4,128,2176]{2,1,0:T(8,128)(2,1)} collective-permute-done((bf16[4,128,2176]{2,1,0:T(8,128)(2,1)}, bf16[4,128,2176]{2,1,0:T(8,128)(2,1)}, u32[]{:S(2)}, u32[]{:S(2)}) %collective-permute-start.36) | collective-permute-done | bytes 2228256 | tf_op jit(solution)/shard_map/ppermute | solution.py:43
  352.4 12.3 %collective-permute-done.37.refs_6_.refs_10_ = bf16[128,2048]{1,0:T(8,128)(2,1)S(1)} collective-permute-done((bf16[128,2048]{1,0:T(8,128)(2,1)S(1)}, bf16[128,2048]{1,0:T(8,128)(2,1)S(1)}, u32[]{:S(2)}, u32[]{:S(2)}) %collective-permute-start.37) | collective-permute-done | bytes 524320 | tf_op jit(solution)/shard_map/ppermute | solution.py:23
  365.3 12.1 %collective-permute-done.44.refs_10_.refs_14_ = bf16[128,2048]{1,0:T(8,128)(2,1)S(1)} collective-permute-done((bf16[128,2048]{1,0:T(8,128)(2,1)S(1)}, bf16[128,2048]{1,0:T(8,128)(2,1)S(1)}, u32[]{:S(2)}, u32[]{:S(2)}) %collective-permute-start.44) | collective-permute-done | bytes 524320 | tf_op jit(solution)/shard_map/ppermute | solution.py:23
  379.7 19.5 %collective-permute-done.39 = bf16[4,128,2176]{2,1,0:T(8,128)(2,1)S(1)} collective-permute-done((bf16[4,128,2176]{2,1,0:T(8,128)(2,1)S(1)}, bf16[4,128,2176]{2,1,0:T(8,128)(2,1)S(1)}, u32[]{:S(2)}, u32[]{:S(2)}) %collective-permute-start.39) | collective-permute-done | bytes 2228256 | tf_op jit(solution)/shard_map/ppermute | solution.py:43
  401.0 10.7 %collective-permute-done.38 = bf16[128,2048]{1,0:T(8,128)(2,1)S(1)} collective-permute-done((bf16[128,2048]{1,0:T(8,128)(2,1)S(1)}, bf16[128,2048]{1,0:T(8,128)(2,1)S(1)}, u32[]{:S(2)}, u32[]{:S(2)}) %collective-permute-start.38) | collective-permute-done | bytes 524320 | tf_op jit(solution)/shard_map/ppermute | solution.py:23
  414.4 18.5 %attend_back.1 = (bf16[4,256,768]{2,1,0:T(8,128)(2,1)}, bf16[4,128,2048]{2,1,0:T(8,128)(2,1)}, bf16[4,128,2048]{2,1,0:T(8,128)(2,1)}) custom-call(s32[4]{0:T(128)} %copy-done.51, f32[4,256,128]{2,1,0:T(8,128)} %pad_maximum_fusion.cosine, f32[4,256,128]{2,1,0:T(8,128)} %pad_maximum_fusion.1.sine, bf16[4,256,256]{2,1,0:T(8,128)(2,1)} %and_convert_fusion.mask, ...), custom_call_target="tpu_custom_call" | custom-call | flops 4966055936 | bytes 8388608 | tf_op jit(solution)/shard_map/attend_back/pallas_call | solution.py:580
  446.7 14.5 %collective-permute-done.52 = bf16[4,128,2176]{2,1,0:T(8,128)(2,1)} collective-permute-done((bf16[4,128,2176]{2,1,0:T(8,128)(2,1)}, bf16[4,128,2176]{2,1,0:T(8,128)(2,1)}, u32[]{:S(2)}, u32[]{:S(2)}) %collective-permute-start.52) | collective-permute-done | bytes 2228256 | tf_op jit(solution)/shard_map/ppermute | solution.py:43
  471.3 9.3 %collective-permute-done.47 = bf16[128,2048]{1,0:T(8,128)(2,1)S(1)} collective-permute-done((bf16[128,2048]{1,0:T(8,128)(2,1)S(1)}, bf16[128,2048]{1,0:T(8,128)(2,1)S(1)}, u32[]{:S(2)}, u32[]{:S(2)}) %collective-permute-start.47) | collective-permute-done | bytes 524320 | tf_op jit(solution)/shard_map/ppermute | solution.py:23
  517.7 8.8 %collective-permute-done.55 = bf16[4,128,512]{2,1,0:T(8,128)(2,1)} collective-permute-done((bf16[4,128,512]{2,1,0:T(8,128)(2,1)}, bf16[4,128,512]{2,1,0:T(8,128)(2,1)}, u32[]{:S(2)}, u32[]{:S(2)}) %collective-permute-start.55) | collective-permute-done | bytes 524320 | tf_op jit(solution)/shard_map/ppermute | solution.py:43
  (307 shorter events, 201.4 us)
Async XLA Ops:
  43.7 42.3 %all-to-all-start = ((bf16[4,128,2176]{2,1,0:T(8,128)(2,1)}), bf16[4,128,2176]{2,1,0:T(8,128)(2,1)}, u32[]{:S(2)}, u32[]{:S(2)}) async-start(bf16[4,128,2176]{2,1,0:T(8,128)(2,1)} %pack_feed.1), calls=%async_computation | async-start | bytes 4456448 | tf_op jit(solution)/shard_map/all_to_all | solution.py:90
  48.2 44.4 %collective-permute-start.5 = (bf16[128,2048]{1,0:T(8,128)(2,1)S(1)}, bf16[128,2048]{1,0:T(8,128)(2,1)S(1)}, u32[]{:S(2)}, u32[]{:S(2)}) collective-permute-start(bf16[128,2048]{1,0:T(8,128)(2,1)S(1)} %multiply_convert_fusion.1.refs_4_.refs_0_), channel_id=1, source_target_pairs={{0,1},{1,0},{2,3},{3,2},{4,5},{5,4},{6,7},{7,6},{8,9},{9,8},{10,11... | collective-permute-start | bytes 1572872 | tf_op jit(solution)/shard_map/ppermute | solution.py:27
  48.3 37.2 %collective-permute-start.7 = (bf16[128,2048]{1,0:T(8,128)(2,1)S(1)}, bf16[128,2048]{1,0:T(8,128)(2,1)S(1)}, u32[]{:S(2)}, u32[]{:S(2)}) collective-permute-start(bf16[128,2048]{1,0:T(8,128)(2,1)S(1)} %multiply_convert_fusion.1.refs_4_.refs_0_), channel_id=1, source_target_pairs={{0,4},{2,6},{4,0},{6,2},{8,12},{10,14},{12,8},{14,10},{16,20},{18,... | collective-permute-start | bytes 1572872 | tf_op jit(solution)/shard_map/ppermute | solution.py:23
  62.5 31.0 %collective-permute-start.6 = (bf16[128,2048]{1,0:T(8,128)(2,1)S(1)}, bf16[128,2048]{1,0:T(8,128)(2,1)}, u32[]{:S(2)}, u32[]{:S(2)}) collective-permute-start(bf16[128,2048]{1,0:T(8,128)(2,1)S(1)} %collective-permute-done.refs_6_.refs_2_), channel_id=1, source_target_pairs={{0,1},{1,0},{2,3},{3,2},{4,5},{5,4},{6,7},{7,6},{8,9},{9,8},{10,11... | collective-permute-start | bytes 1572872 | tf_op jit(solution)/shard_map/ppermute | solution.py:27
  87.1 27.3 %collective-permute-start.4 = (bf16[4,128,1024]{2,1,0:T(8,128)(2,1)}, bf16[4,128,1024]{2,1,0:T(8,128)(2,1)}, u32[]{:S(2)}, u32[]{:S(2)}) collective-permute-start(bf16[4,128,1024]{2,1,0:T(8,128)(2,1)} %collective-permute-done.3.refs_2_), channel_id=1, source_target_pairs={{0,8},{2,10},{4,12},{6,14},{8,24},{10,26},{12,28},{14,30},{24,16},... | collective-permute-start | bytes 3145736 | tf_op jit(solution)/shard_map/ppermute | solution.py:43
  92.6 68.5 %collective-permute-start.16 = (bf16[4,128,2176]{2,1,0:T(8,128)(2,1)}, bf16[4,128,2176]{2,1,0:T(8,128)(2,1)}, u32[]{:S(2)}, u32[]{:S(2)}) collective-permute-start(bf16[4,128,2176]{2,1,0:T(8,128)(2,1)} %all-to-all-done.refs_0_), channel_id=1, source_target_pairs={{0,8},{2,10},{4,12},{6,14},{8,24},{10,26},{12,28},{14,30},{24,16},... | collective-permute-start | bytes 6684680 | tf_op jit(solution)/shard_map/ppermute | solution.py:43
  130.1 31.1 %collective-permute-start.10 = (bf16[4,128,2048]{2,1,0:T(8,128)(2,1)}, bf16[4,128,2048]{2,1,0:T(8,128)(2,1)}, u32[]{:S(2)}, u32[]{:S(2)}) collective-permute-start(bf16[4,128,2048]{2,1,0:T(8,128)(2,1)} %get-tuple-element.81), channel_id=1, source_target_pairs={{0,1},{1,0},{2,3},{3,2},{4,5},{5,4},{6,7},{7,6},{8,9},{9,8},{10,11... | collective-permute-start | bytes 6291464 | tf_op jit(solution)/shard_map/ppermute | solution.py:27
  135.1 28.4 %collective-permute-start.11 = (bf16[128,2048]{1,0:T(8,128)(2,1)S(1)}, bf16[128,2048]{1,0:T(8,128)(2,1)S(1)}, u32[]{:S(2)}, u32[]{:S(2)}) collective-permute-start(bf16[128,2048]{1,0:T(8,128)(2,1)S(1)} %bitcast.63), channel_id=1, source_target_pairs={{0,2},{2,0},{4,6},{6,4},{8,10},{10,8},{12,14},{14,12},{16,18},{18,... | collective-permute-start | bytes 1572872 | tf_op jit(solution)/shard_map/ppermute | solution.py:23
  161.1 50.6 %collective-permute-start.17 = (bf16[4,128,2176]{2,1,0:T(8,128)(2,1)}, bf16[4,128,2176]{2,1,0:T(8,128)(2,1)S(1)}, u32[]{:S(2)}, u32[]{:S(2)}) collective-permute-start(bf16[4,128,2176]{2,1,0:T(8,128)(2,1)} %collective-permute-done.16.refs_1_), channel_id=1, source_target_pairs={{0,8},{2,10},{4,12},{6,14},{8,24},{10,26},{12,28},{14,30},{24,16},... | collective-permute-start | bytes 6684680 | tf_op jit(solution)/shard_map/ppermute | solution.py:43
  180.1 33.1 %collective-permute-start.27 = (bf16[128,2048]{1,0:T(8,128)(2,1)S(1)}, bf16[128,2048]{1,0:T(8,128)(2,1)S(1)}, u32[]{:S(2)}, u32[]{:S(2)}) collective-permute-start(bf16[128,2048]{1,0:T(8,128)(2,1)S(1)} %bitcast.65), channel_id=1, source_target_pairs={{0,1},{1,0},{2,3},{3,2},{4,5},{5,4},{6,7},{7,6},{8,9},{9,8},{10,11... | collective-permute-start | bytes 1572872 | tf_op jit(solution)/shard_map/ppermute | solution.py:27
  180.1 32.0 %collective-permute-start.19 = (bf16[128,2048]{1,0:T(8,128)(2,1)S(1)}, bf16[128,2048]{1,0:T(8,128)(2,1)S(1)}, u32[]{:S(2)}, u32[]{:S(2)}) collective-permute-start(bf16[128,2048]{1,0:T(8,128)(2,1)S(1)} %collective-permute-done.11.refs_14_.refs_10_), channel_id=1, source_target_pairs={{0,4},{2,6},{4,0},{6,2},{8,12},{10,14},{12,8},{14,10},{16,20},{18,... | collective-permute-start | bytes 1572872 | tf_op jit(solution)/shard_map/ppermute | solution.py:23
  211.7 49.8 %collective-permute-start.18 = (bf16[4,128,2176]{2,1,0:T(8,128)(2,1)S(1)}, bf16[4,128,2176]{2,1,0:T(8,128)(2,1)}, u32[]{:S(2)}, u32[]{:S(2)}) collective-permute-start(bf16[4,128,2176]{2,1,0:T(8,128)(2,1)S(1)} %collective-permute-done.17.refs_2_), channel_id=1, source_target_pairs={{0,8},{2,10},{4,12},{6,14},{8,24},{10,26},{12,28},{14,30},{24,16},... | collective-permute-start | bytes 6684680 | tf_op jit(solution)/shard_map/ppermute | solution.py:43
  292.9 52.5 %collective-permute-start.36 = (bf16[4,128,2176]{2,1,0:T(8,128)(2,1)}, bf16[4,128,2176]{2,1,0:T(8,128)(2,1)}, u32[]{:S(2)}, u32[]{:S(2)}) collective-permute-start(bf16[4,128,2176]{2,1,0:T(8,128)(2,1)} %get-tuple-element.99), channel_id=1, source_target_pairs={{0,8},{2,10},{4,12},{6,14},{8,24},{10,26},{12,28},{14,30},{24,16},... | collective-permute-start | bytes 6684680 | tf_op jit(solution)/shard_map/ppermute | solution.py:43
  317.2 31.1 %collective-permute-start.35 = (bf16[128,2048]{1,0:T(8,128)(2,1)}, bf16[128,2048]{1,0:T(8,128)(2,1)S(1)}, u32[]{:S(2)}, u32[]{:S(2)}) collective-permute-start(bf16[128,2048]{1,0:T(8,128)(2,1)} %get-tuple-element.98), channel_id=1, source_target_pairs={{0,4},{2,6},{4,0},{6,2},{8,12},{10,14},{12,8},{14,10},{16,20},{18,... | collective-permute-start | bytes 1572872 | tf_op jit(solution)/shard_map/ppermute | solution.py:23
  319.2 29.1 %collective-permute-start.34 = (bf16[128,2048]{1,0:T(8,128)(2,1)}, bf16[128,2048]{1,0:T(8,128)(2,1)S(1)}, u32[]{:S(2)}, u32[]{:S(2)}) collective-permute-start(bf16[128,2048]{1,0:T(8,128)(2,1)} %fusion), channel_id=1, source_target_pairs={{0,2},{2,0},{4,6},{6,4},{8,10},{10,8},{12,14},{14,12},{16,18},{18,... | collective-permute-start | bytes 1572872 | tf_op jit(solution)/shard_map/ppermute | solution.py:23
  328.6 48.7 %collective-permute-start.33 = (bf16[4,128,2048]{2,1,0:T(8,128)(2,1)}, bf16[4,128,2048]{2,1,0:T(8,128)(2,1)S(1)}, u32[]{:S(2)}, u32[]{:S(2)}) collective-permute-start(bf16[4,128,2048]{2,1,0:T(8,128)(2,1)} %get-tuple-element.93), channel_id=1, source_target_pairs={{0,1},{1,0},{2,3},{3,2},{4,5},{5,4},{6,7},{7,6},{8,9},{9,8},{10,11... | collective-permute-start | bytes 6291464 | tf_op jit(solution)/shard_map/ppermute | solution.py:27
  348.2 50.9 %collective-permute-start.39 = (bf16[4,128,2176]{2,1,0:T(8,128)(2,1)S(1)}, bf16[4,128,2176]{2,1,0:T(8,128)(2,1)S(1)}, u32[]{:S(2)}, u32[]{:S(2)}) collective-permute-start(bf16[4,128,2176]{2,1,0:T(8,128)(2,1)S(1)} %add_convert_fusion.2), channel_id=1, source_target_pairs={{0,8},{2,10},{4,12},{6,14},{8,24},{10,26},{12,28},{14,30},{24,16},... | collective-permute-start | bytes 6684680 | tf_op jit(solution)/shard_map/ppermute | solution.py:43
  364.7 48.1 %collective-permute-start.40 = (bf16[128,2048]{1,0:T(8,128)(2,1)S(1)}, bf16[128,2048]{1,0:T(8,128)(2,1)S(1)}, u32[]{:S(2)}, u32[]{:S(2)}) collective-permute-start(bf16[128,2048]{1,0:T(8,128)(2,1)S(1)} %get-tuple-element.100.refs_4_.refs_8_), channel_id=1, source_target_pairs={{0,1},{1,0},{2,3},{3,2},{4,5},{5,4},{6,7},{7,6},{8,9},{9,8},{10,11... | collective-permute-start | bytes 1572872 | tf_op jit(solution)/shard_map/ppermute | solution.py:27
  364.9 47.9 %collective-permute-start.41 = (bf16[128,2048]{1,0:T(8,128)(2,1)S(1)}, bf16[128,2048]{1,0:T(8,128)(2,1)S(1)}, u32[]{:S(2)}, u32[]{:S(2)}) collective-permute-start(bf16[128,2048]{1,0:T(8,128)(2,1)S(1)} %collective-permute-done.37.refs_6_.refs_10_), channel_id=1, source_target_pairs={{0,1},{1,0},{2,3},{3,2},{4,5},{5,4},{6,7},{7,6},{8,9},{9,8},{10,11... | collective-permute-start | bytes 1572872 | tf_op jit(solution)/shard_map/ppermute | solution.py:27
  377.3 35.5 %collective-permute-start.43 = (bf16[128,2048]{1,0:T(8,128)(2,1)S(1)}, bf16[128,2048]{1,0:T(8,128)(2,1)S(1)}, u32[]{:S(2)}, u32[]{:S(2)}) collective-permute-start(bf16[128,2048]{1,0:T(8,128)(2,1)S(1)} %collective-permute-done.42.refs_8_.refs_12_), channel_id=1, source_target_pairs={{0,1},{1,0},{2,3},{3,2},{4,5},{5,4},{6,7},{7,6},{8,9},{9,8},{10,11... | collective-permute-start | bytes 1572872 | tf_op jit(solution)/shard_map/ppermute | solution.py:27
  377.3 35.6 %collective-permute-start.45 = (bf16[128,2048]{1,0:T(8,128)(2,1)S(1)}, bf16[128,2048]{1,0:T(8,128)(2,1)S(1)}, u32[]{:S(2)}, u32[]{:S(2)}) collective-permute-start(bf16[128,2048]{1,0:T(8,128)(2,1)S(1)} %collective-permute-done.44.refs_10_.refs_14_), channel_id=1, source_target_pairs={{0,1},{1,0},{2,3},{3,2},{4,5},{5,4},{6,7},{7,6},{8,9},{9,8},{10,11... | collective-permute-start | bytes 1572872 | tf_op jit(solution)/shard_map/ppermute | solution.py:27
  411.7 49.5 %collective-permute-start.52 = (bf16[4,128,2176]{2,1,0:T(8,128)(2,1)}, bf16[4,128,2176]{2,1,0:T(8,128)(2,1)}, u32[]{:S(2)}, u32[]{:S(2)}) collective-permute-start(bf16[4,128,2176]{2,1,0:T(8,128)(2,1)} %add_convert_fusion.1), channel_id=1, source_target_pairs={{0,8},{2,10},{4,12},{6,14},{8,24},{10,26},{12,28},{14,30},{24,16},... | collective-permute-start | bytes 6684680 | tf_op jit(solution)/shard_map/ppermute | solution.py:43
  433.0 29.5 %collective-permute-start.46 = (bf16[4,128,2048]{2,1,0:T(8,128)(2,1)}, bf16[4,128,2048]{2,1,0:T(8,128)(2,1)}, u32[]{:S(2)}, u32[]{:S(2)}) collective-permute-start(bf16[4,128,2048]{2,1,0:T(8,128)(2,1)} %get-tuple-element.111), channel_id=1, source_target_pairs={{0,1},{1,0},{2,3},{3,2},{4,5},{5,4},{6,7},{7,6},{8,9},{9,8},{10,11... | collective-permute-start | bytes 6291464 | tf_op jit(solution)/shard_map/ppermute | solution.py:27
  496.3 32.2 %all-to-all-start.2 = ((bf16[4,128,2176]{2,1,0:T(8,128)(2,1)}), bf16[4,128,2176]{2,1,0:T(8,128)(2,1)}, u32[]{:S(2)}, u32[]{:S(2)}) async-start(bf16[4,128,2176]{2,1,0:T(8,128)(2,1)} %add_convert_fusion), calls=%async_computation.2 | async-start | bytes 4456448 | tf_op jit(solution)/shard_map/all_to_all | solution.py:90
  (94 other events, 1519.4 us)

commit v2 on v1

--- a/solution.py
+++ b/solution.py
@@ -62,9 +62,9 @@
     return pieces, tuple(moves)
 
 
-def gather(own):
+def gather(own, *before):
     x, y = over_dp(own, X), over_dp(own, Y)
-    return [own, x, y, over_dp(x, Y)]
+    return [own, x, y, over_dp(after(x, *before), Y)]
 
 
 def plus(base, more):
@@ -693,9 +693,9 @@
         jax.ShapeDtypeStruct((GROUP, shard_rows, 4 * own_width), BF),
     )
     head_own = swap_members(head_packed)
-    blocks_one = gather(after(normed_one.astype(BF), head_packed))
+    head_mats = outer_gather(head_own)
+    blocks_one = gather(normed_one.astype(BF), head_mats[1])
     rows_one = part_of(with_other_core(blocks_one), 0, rows)
-    head_mats = outer_gather(head_own)
     gate_up_flat = gate_up_weight.reshape(shard_rows, 2 * GROUP * own_hidden)
     spare = up_to_lanes(3 * own_hidden) - 3 * own_hidden
     docs = doc_lengths.shape[1]
@@ -711,7 +711,7 @@
         ],
         jax.ShapeDtypeStruct((GROUP, shard_rows, 3 * own_hidden + spare), BF),
     )
-    feed_own = swap_members(after(feed_packed, blocks_one[3]))
+    feed_own = swap_members(after(feed_packed, blocks_one[1]))
     notes = feed_own[:, 0, 3 * own_hidden : 3 * own_hidden + docs].astype(F32)
     chosen = (jnp.arange(GROUP, dtype=jnp.int32)[None, :] == places[:, None])[:, :, None]
     lengths = jnp.sum(jnp.where(chosen, notes[None], 0.0), axis=1).astype(jnp.int32)

time: 579 us -> 572 us (0.988)
  waiting for transfers between devices: 310 us -> 297 us
  starting transfers between devices: 53.3 us -> 62.1 us
    ppermute x15, waiting for transfers between devices: 163 us -> 140 us  [over_ring(): lax.ppermute(x, 'dp', [(GROUP * a + i, GROUP * b + i) for a, b in pairs f...]
    ppermute x24, waiting for transfers between devices: 130 us -> 140 us  [over_dp(): return lax.ppermute(x, 'dp', [(i, i ^ bit) for i in range(size)])]
    ppermute x24, starting transfers between devices: 21.6 us -> 31.7 us  [over_dp(): return lax.ppermute(x, 'dp', [(i, i ^ bit) for i in range(size)])]
  transfers between devices with their start and end apart: 66 -> 66, of which waited for: 29 -> 32; matrix products, arithmetic and copies ran while one was open for 12% -> 13% of each run, Pallas kernels for 15% -> 15%
where the time goes in v2:
time: 572 us; the launch traced here: 562 us
  waiting for transfers between devices  297 us (52%)
  Pallas kernels  118 us (21%)
  starting transfers between devices  62.1 us (11%)
  other arithmetic  51.1 us (9%)
  local copies, waits for them, and re-layouts  31.9 us (6%)
    ppermute x24, waiting for transfers between devices, over_dp(): return lax.ppermute(x, 'dp', [(i, i ^ bit) for i in range(size)])  140 us
    ppermute x15, waiting for transfers between devices, over_ring(): lax.ppermute(x, 'dp', [(GROUP * a + i, GROUP * b + i) for a, b in pairs f...  140 us
    ppermute x24, starting transfers between devices, over_dp(): return lax.ppermute(x, 'dp', [(i, i ^ bit) for i in range(size)])  31.7 us
    pallas_call x1, Pallas kernels, feed(): pl.pallas_call(functools.partial(feed_kernel, moves, cot_moves, outer), g...  31.3 us
    convert_element_type x16, other arithmetic, plus(): return (base.astype(F32) + more.astype(F32)).astype(BF)  31.1 us
    pallas_call x3, Pallas kernels, weight_grads(): pl.pallas_call(functools.partial(grads_kernel, [moves for _, moves in lef...  27.8 us
    all_to_all x5, starting transfers between devices, swap_members(): lax.all_to_all(blocks, 'dp', split_axis=0, concat_axis=0, tiled=True, axi...  21.5 us
    pallas_call x1, Pallas kernels, attend_back(): pl.pallas_call(functools.partial(attend_back_kernel, moves, shard_rows, o...  18.5 us
  transfers between devices with their start and end apart: 66, of which 32 were waited for; matrix products, arithmetic and copies ran while one was open for 13% of the time, Pallas kernels for 15%

profile of v2, /device:TPU:24, one launch (start us, length us, event | category | flops | bytes accessed | tf_op | source)
XLA Modules:
  0.0 562.3 jit_solution(15293174244558306413)
XLA Ops:
  50.5 26.9 %collective-permute-done.6.refs_8_.refs_4_ = bf16[128,2048]{1,0:T(8,128)(2,1)S(1)} collective-permute-done((bf16[128,2048]{1,0:T(8,128)(2,1)S(1)}, bf16[128,2048]{1,0:T(8,128)(2,1)S(1)}, u32[]{:S(2)}, u32[]{:S(2)}) %collective-permute-start.6) | collective-permute-done | bytes 524320 | tf_op jit(solution)/shard_map/ppermute | solution.py:23
  80.5 11.4 %collective-permute-done.8.refs_10_.refs_6_ = bf16[128,2048]{1,0:T(8,128)(2,1)} collective-permute-done((bf16[128,2048]{1,0:T(8,128)(2,1)S(1)}, bf16[128,2048]{1,0:T(8,128)(2,1)}, u32[]{:S(2)}, u32[]{:S(2)}) %collective-permute-start.8) | collective-permute-done | bytes 524320 | tf_op jit(solution)/shard_map/ppermute | solution.py:23
  96.3 9.8 %collective-permute-done.3.refs_3_ = bf16[4,128,1024]{2,1,0:T(8,128)(2,1)} collective-permute-done((bf16[4,128,1024]{2,1,0:T(8,128)(2,1)}, bf16[4,128,1024]{2,1,0:T(8,128)(2,1)}, u32[]{:S(2)}, u32[]{:S(2)}) %collective-permute-start.3) | collective-permute-done | bytes 1048608 | tf_op jit(solution)/shard_map/ppermute | solution.py:43
  106.1 15.7 %attend.1 = (bf16[4,128,2048]{2,1,0:T(8,128)(2,1)}, bf16[4,128,2048]{2,1,0:T(8,128)(2,1)}, bf16[4,256,256]{2,1,0:T(8,128)(2,1)}, bf16[4,256,256]{2,1,0:T(8,128)(...) custom-call(s32[4]{0:T(128)} %copy-done.52, f32[4,256,128]{2,1,0:T(8,128)} %pad_maximum_fusion.cosine, ...), custom_call_target="tpu_custom_call" | custom-call | flops 4563402752 | bytes 8388608 | tf_op jit(solution)/shard_map/attend/pallas_call | solution.py:250
  122.3 30.8 %collective-permute-done.16.refs_1_ = bf16[4,128,2176]{2,1,0:T(8,128)(2,1)} collective-permute-done((bf16[4,128,2176]{2,1,0:T(8,128)(2,1)}, bf16[4,128,2176]{2,1,0:T(8,128)(2,1)}, u32[]{:S(2)}, u32[]{:S(2)}) %collective-permute-start.16) | collective-permute-done | bytes 2228256 | tf_op jit(solution)/shard_map/ppermute | solution.py:43
  173.7 12.8 %collective-permute-done.13 = bf16[128,2048]{1,0:T(8,128)(2,1)S(1)} collective-permute-done((bf16[128,2048]{1,0:T(8,128)(2,1)S(1)}, bf16[128,2048]{1,0:T(8,128)(2,1)S(1)}, u32[]{:S(2)}, u32[]{:S(2)}) %collective-permute-start.13) | collective-permute-done | bytes 524320 | tf_op jit(solution)/shard_map/ppermute | solution.py:23
  188.8 15.6 %collective-permute-done.17.refs_2_ = bf16[4,128,2176]{2,1,0:T(8,128)(2,1)} collective-permute-done((bf16[4,128,2176]{2,1,0:T(8,128)(2,1)}, bf16[4,128,2176]{2,1,0:T(8,128)(2,1)}, u32[]{:S(2)}, u32[]{:S(2)}) %collective-permute-start.17) | collective-permute-done | bytes 2228256 | tf_op jit(solution)/shard_map/ppermute | solution.py:43
  207.4 10.0 %collective-permute-done.21.refs_6_.refs_2_ = bf16[128,2048]{1,0:T(8,128)(2,1)S(1)} collective-permute-done((bf16[128,2048]{1,0:T(8,128)(2,1)S(1)}, bf16[128,2048]{1,0:T(8,128)(2,1)S(1)}, u32[]{:S(2)}, u32[]{:S(2)}) %collective-permute-start.21) | collective-permute-done | bytes 524320 | tf_op jit(solution)/shard_map/ppermute | solution.py:23
  220.1 12.2 %collective-permute-done.23.refs_8_.refs_4_ = bf16[128,2048]{1,0:T(8,128)(2,1)S(1)} collective-permute-done((bf16[128,2048]{1,0:T(8,128)(2,1)S(1)}, bf16[128,2048]{1,0:T(8,128)(2,1)S(1)}, u32[]{:S(2)}, u32[]{:S(2)}) %collective-permute-start.23) | collective-permute-done | bytes 524320 | tf_op jit(solution)/shard_map/ppermute | solution.py:23
  232.3 10.8 %collective-permute-done.25.refs_10_.refs_6_ = bf16[128,2048]{1,0:T(8,128)(2,1)S(1)} collective-permute-done((bf16[128,2048]{1,0:T(8,128)(2,1)S(1)}, bf16[128,2048]{1,0:T(8,128)(2,1)S(1)}, u32[]{:S(2)}, u32[]{:S(2)}) %collective-permute-start.25) | collective-permute-done | bytes 524320 | tf_op jit(solution)/shard_map/ppermute | solution.py:23
  245.8 8.6 %collective-permute-done.18.refs_3_ = bf16[4,128,2176]{2,1,0:T(8,128)(2,1)} collective-permute-done((bf16[4,128,2176]{2,1,0:T(8,128)(2,1)}, bf16[4,128,2176]{2,1,0:T(8,128)(2,1)}, u32[]{:S(2)}, u32[]{:S(2)}) %collective-permute-start.18) | collective-permute-done | bytes 2228256 | tf_op jit(solution)/shard_map/ppermute | solution.py:43
  254.4 31.3 %feed.1 = (bf16[4,128,2048]{2,1,0:T(8,128)(2,1)}, bf16[4,128,2048]{2,1,0:T(8,128)(2,1)}, bf16[4,256,768]{2,1,0:T(8,128)(2,1)}, bf16[4,256,1408]{2,1,0:T(8,128)(2,1)}, bf16[4,128,2176]{2,1,0:T(8,128)(2,1)}) custom-call(s32[4]{0:T(128)} %copy-done.52, bf16[4,128,2176]{2,1,0:T(8,128)(2,1)} %all-to-all-done.refs_0_, ...), custom_call_target="tpu_custom_call" | custom-call | flops 14763950080 | bytes 12582912 | tf_op jit(solution)/shard_map/feed/pallas_call | solution.py:336
  295.4 14.2 %weight_grads.3 = (bf16[4,128,2176]{2,1,0:T(8,128)(2,1)}, bf16[4,128,2176]{2,1,0:T(8,128)(2,1)}, bf16[4,128,2176]{2,1,0:T(8,128)(2,1)}) custom-call(bf16[128,2048]{1,0:T(8,128)(2,1)} %copy-done.32, bf16[128,2048]{1,0:T(8,128)(2,1)} %copy-done.45, bf16[128,2048]{1,0:T(8,128)(2,1)} %copy-done.37, bf16[128,2048]{1,0:T(8,128)(2,1)} %copy-done.46, ...), custom_call_target="tpu_custom_call" | custom-call | flops 6845104128 | bytes 3145728 | tf_op jit(solution)/shard_map/weight_grads/pallas_call | solution.py:448
  313.8 9.0 %feed_out.1 = (bf16[4,128,2048]{2,1,0:T(8,128)(2,1)}, bf16[4,128,2048]{2,1,0:T(8,128)(2,1)}) custom-call(s32[4]{0:T(128)} %copy-done.52, bf16[4,256,768]{2,1,0:T(8,128)(2,1)} %get-tuple-element.91.hidden.refs_17_, bf16[4,128,2176]{2,1,0:T(8,128)(2,1)} %all-to-all-done.refs_0_, bf16[4,128,2176]{2,1,0:T(8,128)(2,1)} %collective-permute-done.16.refs_1_, ...), custom_call_target="tpu_custom_call" | custom-call | flops 2952790016 | bytes 8388608 | tf_op jit(solution)/shard_map/feed_out/pallas_call | solution.py:382
  322.8 15.2 %collective-permute-done.36 = bf16[4,128,2176]{2,1,0:T(8,128)(2,1)} collective-permute-done((bf16[4,128,2176]{2,1,0:T(8,128)(2,1)}, bf16[4,128,2176]{2,1,0:T(8,128)(2,1)}, u32[]{:S(2)}, u32[]{:S(2)}) %collective-permute-start.36) | collective-permute-done | bytes 2228256 | tf_op jit(solution)/shard_map/ppermute | solution.py:43
  347.1 10.3 %collective-permute-done.37.refs_6_.refs_10_ = bf16[128,2048]{1,0:T(8,128)(2,1)S(1)} collective-permute-done((bf16[128,2048]{1,0:T(8,128)(2,1)S(1)}, bf16[128,2048]{1,0:T(8,128)(2,1)S(1)}, u32[]{:S(2)}, u32[]{:S(2)}) %collective-permute-start.37) | collective-permute-done | bytes 524320 | tf_op jit(solution)/shard_map/ppermute | solution.py:23
  359.6 10.4 %collective-permute-done.44.refs_10_.refs_14_ = bf16[128,2048]{1,0:T(8,128)(2,1)S(1)} collective-permute-done((bf16[128,2048]{1,0:T(8,128)(2,1)S(1)}, bf16[128,2048]{1,0:T(8,128)(2,1)S(1)}, u32[]{:S(2)}, u32[]{:S(2)}) %collective-permute-start.44) | collective-permute-done | bytes 524320 | tf_op jit(solution)/shard_map/ppermute | solution.py:23
  372.4 19.4 %collective-permute-done.39 = bf16[4,128,2176]{2,1,0:T(8,128)(2,1)S(1)} collective-permute-done((bf16[4,128,2176]{2,1,0:T(8,128)(2,1)S(1)}, bf16[4,128,2176]{2,1,0:T(8,128)(2,1)S(1)}, u32[]{:S(2)}, u32[]{:S(2)}) %collective-permute-start.39) | collective-permute-done | bytes 2228256 | tf_op jit(solution)/shard_map/ppermute | solution.py:43
  395.4 9.0 %collective-permute-done.38 = bf16[128,2048]{1,0:T(8,128)(2,1)S(1)} collective-permute-done((bf16[128,2048]{1,0:T(8,128)(2,1)S(1)}, bf16[128,2048]{1,0:T(8,128)(2,1)S(1)}, u32[]{:S(2)}, u32[]{:S(2)}) %collective-permute-start.38) | collective-permute-done | bytes 524320 | tf_op jit(solution)/shard_map/ppermute | solution.py:23
  407.1 18.5 %attend_back.1 = (bf16[4,256,768]{2,1,0:T(8,128)(2,1)}, bf16[4,128,2048]{2,1,0:T(8,128)(2,1)}, bf16[4,128,2048]{2,1,0:T(8,128)(2,1)}) custom-call(s32[4]{0:T(128)} %copy-done.52, f32[4,256,128]{2,1,0:T(8,128)} %pad_maximum_fusion.cosine, f32[4,256,128]{2,1,0:T(8,128)} %pad_maximum_fusion.1.sine, bf16[4,256,256]{2,1,0:T(8,128)(2,1)} %and_convert_fusion.mask, ...), custom_call_target="tpu_custom_call" | custom-call | flops 4966055936 | bytes 8388608 | tf_op jit(solution)/shard_map/attend_back/pallas_call | solution.py:580
  431.1 8.3 %weight_grads.5 = (bf16[4,128,512]{2,1,0:T(8,128)(2,1)}, bf16[4,128,512]{2,1,0:T(8,128)(2,1)}, bf16[4,128,512]{2,1,0:T(8,128)(2,1)}, bf16[4,128,512]{2,1,0:T(8,1...) custom-call(bf16[128,2048]{1,0:T(8,128)(2,1)} %copy-done.7, bf16[128,2048]{1,0:T(8,128)(2,1)} %copy-done.16, ...), custom_call_target="tpu_custom_call" | custom-call | flops 3221225472 | bytes 3145728 | tf_op jit(solution)/shard_map/weight_grads/pallas_call | solution.py:448
  439.4 14.5 %collective-permute-done.52 = bf16[4,128,2176]{2,1,0:T(8,128)(2,1)} collective-permute-done((bf16[4,128,2176]{2,1,0:T(8,128)(2,1)}, bf16[4,128,2176]{2,1,0:T(8,128)(2,1)}, u32[]{:S(2)}, u32[]{:S(2)}) %collective-permute-start.52) | collective-permute-done | bytes 2228256 | tf_op jit(solution)/shard_map/ppermute | solution.py:43
  463.6 9.3 %collective-permute-done.47 = bf16[128,2048]{1,0:T(8,128)(2,1)S(1)} collective-permute-done((bf16[128,2048]{1,0:T(8,128)(2,1)S(1)}, bf16[128,2048]{1,0:T(8,128)(2,1)S(1)}, u32[]{:S(2)}, u32[]{:S(2)}) %collective-permute-start.47) | collective-permute-done | bytes 524320 | tf_op jit(solution)/shard_map/ppermute | solution.py:23
  510.5 10.3 %collective-permute-done.55 = bf16[4,128,512]{2,1,0:T(8,128)(2,1)} collective-permute-done((bf16[4,128,512]{2,1,0:T(8,128)(2,1)}, bf16[4,128,512]{2,1,0:T(8,128)(2,1)}, u32[]{:S(2)}, u32[]{:S(2)}) %collective-permute-start.55) | collective-permute-done | bytes 524320 | tf_op jit(solution)/shard_map/ppermute | solution.py:43
  (309 shorter events, 215.8 us)
Async XLA Ops:
  36.0 41.9 %all-to-all-start = ((bf16[4,128,2176]{2,1,0:T(8,128)(2,1)}), bf16[4,128,2176]{2,1,0:T(8,128)(2,1)}, u32[]{:S(2)}, u32[]{:S(2)}) async-start(bf16[4,128,2176]{2,1,0:T(8,128)(2,1)} %pack_feed.1), calls=%async_computation | async-start | bytes 4456448 | tf_op jit(solution)/shard_map/all_to_all | solution.py:90
  40.4 54.3 %collective-permute-start.4 = (bf16[128,2048]{1,0:T(8,128)(2,1)S(1)}, bf16[128,2048]{1,0:T(8,128)(2,1)S(1)}, u32[]{:S(2)}, u32[]{:S(2)}) collective-permute-start(bf16[128,2048]{1,0:T(8,128)(2,1)S(1)} %multiply_convert_fusion.1.refs_4_.refs_0_), channel_id=1, source_target_pairs={{0,1},{1,0},{2,3},{3,2},{4,5},{5,4},{6,7},{7,6},{8,9},{9,8},{10,11... | collective-permute-start | bytes 1572872 | tf_op jit(solution)/shard_map/ppermute | solution.py:27
  40.5 36.9 %collective-permute-start.6 = (bf16[128,2048]{1,0:T(8,128)(2,1)S(1)}, bf16[128,2048]{1,0:T(8,128)(2,1)S(1)}, u32[]{:S(2)}, u32[]{:S(2)}) collective-permute-start(bf16[128,2048]{1,0:T(8,128)(2,1)S(1)} %multiply_convert_fusion.1.refs_4_.refs_0_), channel_id=1, source_target_pairs={{0,4},{2,6},{4,0},{6,2},{8,12},{10,14},{12,8},{14,10},{16,20},{18,... | collective-permute-start | bytes 1572872 | tf_op jit(solution)/shard_map/ppermute | solution.py:23
  50.1 28.7 %collective-permute-start.2 = (bf16[4,128,1024]{2,1,0:T(8,128)(2,1)}, bf16[4,128,1024]{2,1,0:T(8,128)(2,1)}, u32[]{:S(2)}, u32[]{:S(2)}) collective-permute-start(bf16[4,128,1024]{2,1,0:T(8,128)(2,1)} %collective-permute-done.1.refs_1_), channel_id=1, source_target_pairs={{0,8},{2,10},{4,12},{6,14},{8,24},{10,26},{12,28},{14,30},{24,16},... | collective-permute-start | bytes 3145736 | tf_op jit(solution)/shard_map/ppermute | solution.py:43
  50.4 45.9 %collective-permute-start.5 = (bf16[128,2048]{1,0:T(8,128)(2,1)S(1)}, bf16[128,2048]{1,0:T(8,128)(2,1)}, u32[]{:S(2)}, u32[]{:S(2)}) collective-permute-start(bf16[128,2048]{1,0:T(8,128)(2,1)S(1)} %collective-permute-done.refs_6_.refs_2_), channel_id=1, source_target_pairs={{0,1},{1,0},{2,3},{3,2},{4,5},{5,4},{6,7},{7,6},{8,9},{9,8},{10,11... | collective-permute-start | bytes 1572872 | tf_op jit(solution)/shard_map/ppermute | solution.py:27
  78.8 27.3 %collective-permute-start.3 = (bf16[4,128,1024]{2,1,0:T(8,128)(2,1)}, bf16[4,128,1024]{2,1,0:T(8,128)(2,1)}, u32[]{:S(2)}, u32[]{:S(2)}) collective-permute-start(bf16[4,128,1024]{2,1,0:T(8,128)(2,1)} %collective-permute-done.2.refs_2_), channel_id=1, source_target_pairs={{0,8},{2,10},{4,12},{6,14},{8,24},{10,26},{12,28},{14,30},{24,16},... | collective-permute-start | bytes 3145736 | tf_op jit(solution)/shard_map/ppermute | solution.py:43
  94.8 58.3 %collective-permute-start.16 = (bf16[4,128,2176]{2,1,0:T(8,128)(2,1)}, bf16[4,128,2176]{2,1,0:T(8,128)(2,1)}, u32[]{:S(2)}, u32[]{:S(2)}) collective-permute-start(bf16[4,128,2176]{2,1,0:T(8,128)(2,1)} %all-to-all-done.refs_0_), channel_id=1, source_target_pairs={{0,8},{2,10},{4,12},{6,14},{8,24},{10,26},{12,28},{14,30},{24,16},... | collective-permute-start | bytes 6684680 | tf_op jit(solution)/shard_map/ppermute | solution.py:43
  121.8 38.4 %collective-permute-start.10 = (bf16[4,128,2048]{2,1,0:T(8,128)(2,1)}, bf16[4,128,2048]{2,1,0:T(8,128)(2,1)}, u32[]{:S(2)}, u32[]{:S(2)}) collective-permute-start(bf16[4,128,2048]{2,1,0:T(8,128)(2,1)} %get-tuple-element.81), channel_id=1, source_target_pairs={{0,1},{1,0},{2,3},{3,2},{4,5},{5,4},{6,7},{7,6},{8,9},{9,8},{10,11... | collective-permute-start | bytes 6291464 | tf_op jit(solution)/shard_map/ppermute | solution.py:27
  153.1 51.3 %collective-permute-start.17 = (bf16[4,128,2176]{2,1,0:T(8,128)(2,1)}, bf16[4,128,2176]{2,1,0:T(8,128)(2,1)}, u32[]{:S(2)}, u32[]{:S(2)}) collective-permute-start(bf16[4,128,2176]{2,1,0:T(8,128)(2,1)} %collective-permute-done.16.refs_1_), channel_id=1, source_target_pairs={{0,8},{2,10},{4,12},{6,14},{8,24},{10,26},{12,28},{14,30},{24,16},... | collective-permute-start | bytes 6684680 | tf_op jit(solution)/shard_map/ppermute | solution.py:43
  173.2 31.3 %collective-permute-start.15 = (bf16[128,2048]{1,0:T(8,128)(2,1)S(1)}, bf16[128,2048]{1,0:T(8,128)(2,1)S(1)}, u32[]{:S(2)}, u32[]{:S(2)}) collective-permute-start(bf16[128,2048]{1,0:T(8,128)(2,1)S(1)} %get-tuple-element.86), channel_id=1, source_target_pairs={{0,4},{2,6},{4,0},{6,2},{8,12},{10,14},{12,8},{14,10},{16,20},{18,... | collective-permute-start | bytes 1572872 | tf_op jit(solution)/shard_map/ppermute | solution.py:23
  204.4 50.0 %collective-permute-start.18 = (bf16[4,128,2176]{2,1,0:T(8,128)(2,1)}, bf16[4,128,2176]{2,1,0:T(8,128)(2,1)}, u32[]{:S(2)}, u32[]{:S(2)}) collective-permute-start(bf16[4,128,2176]{2,1,0:T(8,128)(2,1)} %collective-permute-done.17.refs_2_), channel_id=1, source_target_pairs={{0,8},{2,10},{4,12},{6,14},{8,24},{10,26},{12,28},{14,30},{24,16},... | collective-permute-start | bytes 6684680 | tf_op jit(solution)/shard_map/ppermute | solution.py:43
  285.8 52.2 %collective-permute-start.36 = (bf16[4,128,2176]{2,1,0:T(8,128)(2,1)}, bf16[4,128,2176]{2,1,0:T(8,128)(2,1)}, u32[]{:S(2)}, u32[]{:S(2)}) collective-permute-start(bf16[4,128,2176]{2,1,0:T(8,128)(2,1)} %get-tuple-element.99), channel_id=1, source_target_pairs={{0,8},{2,10},{4,12},{6,14},{8,24},{10,26},{12,28},{14,30},{24,16},... | collective-permute-start | bytes 6684680 | tf_op jit(solution)/shard_map/ppermute | solution.py:43
  311.8 29.1 %collective-permute-start.35 = (bf16[128,2048]{1,0:T(8,128)(2,1)}, bf16[128,2048]{1,0:T(8,128)(2,1)S(1)}, u32[]{:S(2)}, u32[]{:S(2)}) collective-permute-start(bf16[128,2048]{1,0:T(8,128)(2,1)} %get-tuple-element.98), channel_id=1, source_target_pairs={{0,4},{2,6},{4,0},{6,2},{8,12},{10,14},{12,8},{14,10},{16,20},{18,... | collective-permute-start | bytes 1572872 | tf_op jit(solution)/shard_map/ppermute | solution.py:23
  312.1 28.9 %collective-permute-start.34 = (bf16[128,2048]{1,0:T(8,128)(2,1)}, bf16[128,2048]{1,0:T(8,128)(2,1)S(1)}, u32[]{:S(2)}, u32[]{:S(2)}) collective-permute-start(bf16[128,2048]{1,0:T(8,128)(2,1)} %fusion), channel_id=1, source_target_pairs={{0,2},{2,0},{4,6},{6,4},{8,10},{10,8},{12,14},{14,12},{16,18},{18,... | collective-permute-start | bytes 1572872 | tf_op jit(solution)/shard_map/ppermute | solution.py:23
  322.8 47.3 %collective-permute-start.33 = (bf16[4,128,2048]{2,1,0:T(8,128)(2,1)}, bf16[4,128,2048]{2,1,0:T(8,128)(2,1)S(1)}, u32[]{:S(2)}, u32[]{:S(2)}) collective-permute-start(bf16[4,128,2048]{2,1,0:T(8,128)(2,1)} %get-tuple-element.93), channel_id=1, source_target_pairs={{0,1},{1,0},{2,3},{3,2},{4,5},{5,4},{6,7},{7,6},{8,9},{9,8},{10,11... | collective-permute-start | bytes 6291464 | tf_op jit(solution)/shard_map/ppermute | solution.py:27
  340.9 50.9 %collective-permute-start.39 = (bf16[4,128,2176]{2,1,0:T(8,128)(2,1)S(1)}, bf16[4,128,2176]{2,1,0:T(8,128)(2,1)S(1)}, u32[]{:S(2)}, u32[]{:S(2)}) collective-permute-start(bf16[4,128,2176]{2,1,0:T(8,128)(2,1)S(1)} %add_convert_fusion.2), channel_id=1, source_target_pairs={{0,8},{2,10},{4,12},{6,14},{8,24},{10,26},{12,28},{14,30},{24,16},... | collective-permute-start | bytes 6684680 | tf_op jit(solution)/shard_map/ppermute | solution.py:43
  359.1 46.4 %collective-permute-start.40 = (bf16[128,2048]{1,0:T(8,128)(2,1)S(1)}, bf16[128,2048]{1,0:T(8,128)(2,1)S(1)}, u32[]{:S(2)}, u32[]{:S(2)}) collective-permute-start(bf16[128,2048]{1,0:T(8,128)(2,1)S(1)} %get-tuple-element.100.refs_4_.refs_8_), channel_id=1, source_target_pairs={{0,1},{1,0},{2,3},{3,2},{4,5},{5,4},{6,7},{7,6},{8,9},{9,8},{10,11... | collective-permute-start | bytes 1572872 | tf_op jit(solution)/shard_map/ppermute | solution.py:27
  359.1 46.4 %collective-permute-start.41 = (bf16[128,2048]{1,0:T(8,128)(2,1)S(1)}, bf16[128,2048]{1,0:T(8,128)(2,1)S(1)}, u32[]{:S(2)}, u32[]{:S(2)}) collective-permute-start(bf16[128,2048]{1,0:T(8,128)(2,1)S(1)} %collective-permute-done.37.refs_6_.refs_10_), channel_id=1, source_target_pairs={{0,1},{1,0},{2,3},{3,2},{4,5},{5,4},{6,7},{7,6},{8,9},{9,8},{10,11... | collective-permute-start | bytes 1572872 | tf_op jit(solution)/shard_map/ppermute | solution.py:27
  370.0 35.5 %collective-permute-start.43 = (bf16[128,2048]{1,0:T(8,128)(2,1)S(1)}, bf16[128,2048]{1,0:T(8,128)(2,1)S(1)}, u32[]{:S(2)}, u32[]{:S(2)}) collective-permute-start(bf16[128,2048]{1,0:T(8,128)(2,1)S(1)} %collective-permute-done.42.refs_8_.refs_12_), channel_id=1, source_target_pairs={{0,1},{1,0},{2,3},{3,2},{4,5},{5,4},{6,7},{7,6},{8,9},{9,8},{10,11... | collective-permute-start | bytes 1572872 | tf_op jit(solution)/shard_map/ppermute | solution.py:27
  370.0 35.5 %collective-permute-start.45 = (bf16[128,2048]{1,0:T(8,128)(2,1)S(1)}, bf16[128,2048]{1,0:T(8,128)(2,1)S(1)}, u32[]{:S(2)}, u32[]{:S(2)}) collective-permute-start(bf16[128,2048]{1,0:T(8,128)(2,1)S(1)} %collective-permute-done.44.refs_10_.refs_14_), channel_id=1, source_target_pairs={{0,1},{1,0},{2,3},{3,2},{4,5},{5,4},{6,7},{7,6},{8,9},{9,8},{10,11... | collective-permute-start | bytes 1572872 | tf_op jit(solution)/shard_map/ppermute | solution.py:27
  404.4 49.6 %collective-permute-start.52 = (bf16[4,128,2176]{2,1,0:T(8,128)(2,1)}, bf16[4,128,2176]{2,1,0:T(8,128)(2,1)}, u32[]{:S(2)}, u32[]{:S(2)}) collective-permute-start(bf16[4,128,2176]{2,1,0:T(8,128)(2,1)} %add_convert_fusion.1), channel_id=1, source_target_pairs={{0,8},{2,10},{4,12},{6,14},{8,24},{10,26},{12,28},{14,30},{24,16},... | collective-permute-start | bytes 6684680 | tf_op jit(solution)/shard_map/ppermute | solution.py:43
  425.6 29.1 %collective-permute-start.46 = (bf16[4,128,2048]{2,1,0:T(8,128)(2,1)}, bf16[4,128,2048]{2,1,0:T(8,128)(2,1)}, u32[]{:S(2)}, u32[]{:S(2)}) collective-permute-start(bf16[4,128,2048]{2,1,0:T(8,128)(2,1)} %get-tuple-element.111), channel_id=1, source_target_pairs={{0,1},{1,0},{2,3},{3,2},{4,5},{5,4},{6,7},{7,6},{8,9},{9,8},{10,11... | collective-permute-start | bytes 6291464 | tf_op jit(solution)/shard_map/ppermute | solution.py:27
  477.9 27.7 %collective-permute-start.49 = (bf16[128,2048]{1,0:T(8,128)(2,1)}, bf16[128,2048]{1,0:T(8,128)(2,1)}, u32[]{:S(2)}, u32[]{:S(2)}) collective-permute-start(bf16[128,2048]{1,0:T(8,128)(2,1)} %get-tuple-element.120), channel_id=1, source_target_pairs={{0,4},{2,6},{4,0},{6,2},{8,12},{10,14},{12,8},{14,10},{16,20},{18,... | collective-permute-start | bytes 1572872 | tf_op jit(solution)/shard_map/ppermute | solution.py:23
  487.5 35.2 %all-to-all-start.2 = ((bf16[4,128,2176]{2,1,0:T(8,128)(2,1)}), bf16[4,128,2176]{2,1,0:T(8,128)(2,1)}, u32[]{:S(2)}, u32[]{:S(2)}) async-start(bf16[4,128,2176]{2,1,0:T(8,128)(2,1)} %add_convert_fusion), calls=%async_computation.2 | async-start | bytes 4456448 | tf_op jit(solution)/shard_map/all_to_all | solution.py:90
  (95 other events, 1461.2 us)

commit v3 on v2

--- a/solution.py
+++ b/solution.py
@@ -758,7 +758,7 @@
         shard_rows,
         cosine,
         sine,
-        after(mask, y_terms[1], feed_sums[1]),
+        after(mask, feed_sums[1]),
         queries,
         keys,
         values,
@@ -766,7 +766,7 @@
     head_args = [rows_one, rows_grad], [grad_qkv, mixed], shard_rows
     widths = [2 * own_width] * 2
     [head_first] = weight_grads(*head_args, ones, widths)
-    head_args = head_args[0], [after(grad_qkv, *head_first), mixed], shard_rows
+    head_args = head_args[0], [after(grad_qkv, *head_first, y_terms[1]), mixed], shard_rows
     head_rest = weight_grads(*head_args, rest, widths)
     terms = reduce_first(after_all(both_cores(m_own, m_other), *head_first))
     back_one = reduce_last(*terms)

time: 572 us -> 577 us (level)
    ppermute x24, waiting for transfers between devices: 140 us -> 126 us  [over_dp(): return lax.ppermute(x, 'dp', [(i, i ^ bit) for i in range(size)])]
    ppermute x15, waiting for transfers between devices: 140 us -> 152 us  [over_ring(): lax.ppermute(x, 'dp', [(GROUP * a + i, GROUP * b + i) for a, b in pairs f...]
    unnamed x113 -> x101, local copies, waits for them, and re-layouts: 10.6 us -> 12 us
  transfers between devices with their start and end apart: 66 -> 66, of which waited for: 32 -> 31; matrix products, arithmetic and copies ran while one was open for 13% -> 14% of each run, Pallas kernels for 15% -> 15%
where the time goes in v3:
time: 577 us; the launch traced here: 566 us
  waiting for transfers between devices  295 us (51%)
  Pallas kernels  118 us (20%)
  starting transfers between devices  61 us (11%)
  other arithmetic  56.1 us (10%)
  local copies, waits for them, and re-layouts  33.3 us (6%)
    ppermute x15, waiting for transfers between devices, over_ring(): lax.ppermute(x, 'dp', [(GROUP * a + i, GROUP * b + i) for a, b in pairs f...  152 us
    ppermute x24, waiting for transfers between devices, over_dp(): return lax.ppermute(x, 'dp', [(i, i ^ bit) for i in range(size)])  126 us
    convert_element_type x16, other arithmetic, plus(): return (base.astype(F32) + more.astype(F32)).astype(BF)  36.6 us
    ppermute x24, starting transfers between devices, over_dp(): return lax.ppermute(x, 'dp', [(i, i ^ bit) for i in range(size)])  31.8 us
    pallas_call x1, Pallas kernels, feed(): pl.pallas_call(functools.partial(feed_kernel, moves, cot_moves, outer), g...  31.3 us
    pallas_call x3, Pallas kernels, weight_grads(): pl.pallas_call(functools.partial(grads_kernel, [moves for _, moves in lef...  27.9 us
    all_to_all x5, starting transfers between devices, swap_members(): lax.all_to_all(blocks, 'dp', split_axis=0, concat_axis=0, tiled=True, axi...  20.2 us
    pallas_call x1, Pallas kernels, attend_back(): pl.pallas_call(functools.partial(attend_back_kernel, moves, shard_rows, o...  18.5 us
  transfers between devices with their start and end apart: 66, of which 31 were waited for; matrix products, arithmetic and copies ran while one was open for 14% of the time, Pallas kernels for 15%

profile of v3, /device:TPU:24, one launch (start us, length us, event | category | flops | bytes accessed | tf_op | source)
XLA Modules:
  0.0 566.0 jit_solution(10340239674516563134)
XLA Ops:
  18.2 7.7 %all-to-all-done.1.refs_0_ = bf16[4,128,1024]{2,1,0:T(8,128)(2,1)} async-done(((bf16[4,128,1024]{2,1,0:T(8,128)(2,1)}), bf16[4,128,1024]{2,1,0:T(8,128)(2,1)}, u32[]{:S(2)}, u32[]{:S(2)}) %all-to-all-start.1) | async-done | bytes 1048608 | tf_op jit(solution)/shard_map/all_to_all | solution.py:90
  42.4 7.7 %collective-permute-done.1.refs_1_ = bf16[4,128,1024]{2,1,0:T(8,128)(2,1)} collective-permute-done((bf16[4,128,1024]{2,1,0:T(8,128)(2,1)}, bf16[4,128,1024]{2,1,0:T(8,128)(2,1)}, u32[]{:S(2)}, u32[]{:S(2)}) %collective-permute-start.1) | collective-permute-done | bytes 1048608 | tf_op jit(solution)/shard_map/ppermute | solution.py:43
  50.5 26.9 %collective-permute-done.6.refs_8_.refs_4_ = bf16[128,2048]{1,0:T(8,128)(2,1)S(1)} collective-permute-done((bf16[128,2048]{1,0:T(8,128)(2,1)S(1)}, bf16[128,2048]{1,0:T(8,128)(2,1)S(1)}, u32[]{:S(2)}, u32[]{:S(2)}) %collective-permute-start.6) | collective-permute-done | bytes 524320 | tf_op jit(solution)/shard_map/ppermute | solution.py:23
  80.5 11.4 %collective-permute-done.8.refs_10_.refs_6_ = bf16[128,2048]{1,0:T(8,128)(2,1)} collective-permute-done((bf16[128,2048]{1,0:T(8,128)(2,1)S(1)}, bf16[128,2048]{1,0:T(8,128)(2,1)}, u32[]{:S(2)}, u32[]{:S(2)}) %collective-permute-start.8) | collective-permute-done | bytes 524320 | tf_op jit(solution)/shard_map/ppermute | solution.py:23
  96.3 9.8 %collective-permute-done.3.refs_3_ = bf16[4,128,1024]{2,1,0:T(8,128)(2,1)} collective-permute-done((bf16[4,128,1024]{2,1,0:T(8,128)(2,1)}, bf16[4,128,1024]{2,1,0:T(8,128)(2,1)}, u32[]{:S(2)}, u32[]{:S(2)}) %collective-permute-start.3) | collective-permute-done | bytes 1048608 | tf_op jit(solution)/shard_map/ppermute | solution.py:43
  106.1 15.7 %attend.1 = (bf16[4,128,2048]{2,1,0:T(8,128)(2,1)}, bf16[4,128,2048]{2,1,0:T(8,128)(2,1)}, bf16[4,256,256]{2,1,0:T(8,128)(2,1)}, bf16[4,256,256]{2,1,0:T(8,128)(...) custom-call(s32[4]{0:T(128)} %copy-done.46, f32[4,256,128]{2,1,0:T(8,128)} %pad_maximum_fusion.cosine, ...), custom_call_target="tpu_custom_call" | custom-call | flops 4563402752 | bytes 8388608 | tf_op jit(solution)/shard_map/attend/pallas_call | solution.py:250
  122.3 30.7 %collective-permute-done.16.refs_1_ = bf16[4,128,2176]{2,1,0:T(8,128)(2,1)} collective-permute-done((bf16[4,128,2176]{2,1,0:T(8,128)(2,1)}, bf16[4,128,2176]{2,1,0:T(8,128)(2,1)}, u32[]{:S(2)}, u32[]{:S(2)}) %collective-permute-start.16) | collective-permute-done | bytes 2228256 | tf_op jit(solution)/shard_map/ppermute | solution.py:43
  173.7 12.8 %collective-permute-done.13 = bf16[128,2048]{1,0:T(8,128)(2,1)S(1)} collective-permute-done((bf16[128,2048]{1,0:T(8,128)(2,1)S(1)}, bf16[128,2048]{1,0:T(8,128)(2,1)S(1)}, u32[]{:S(2)}, u32[]{:S(2)}) %collective-permute-start.13) | collective-permute-done | bytes 524320 | tf_op jit(solution)/shard_map/ppermute | solution.py:23
  188.8 15.6 %collective-permute-done.17.refs_2_ = bf16[4,128,2176]{2,1,0:T(8,128)(2,1)} collective-permute-done((bf16[4,128,2176]{2,1,0:T(8,128)(2,1)}, bf16[4,128,2176]{2,1,0:T(8,128)(2,1)}, u32[]{:S(2)}, u32[]{:S(2)}) %collective-permute-start.17) | collective-permute-done | bytes 2228256 | tf_op jit(solution)/shard_map/ppermute | solution.py:43
  207.4 10.0 %collective-permute-done.21.refs_6_.refs_2_ = bf16[128,2048]{1,0:T(8,128)(2,1)S(1)} collective-permute-done((bf16[128,2048]{1,0:T(8,128)(2,1)S(1)}, bf16[128,2048]{1,0:T(8,128)(2,1)S(1)}, u32[]{:S(2)}, u32[]{:S(2)}) %collective-permute-start.21) | collective-permute-done | bytes 524320 | tf_op jit(solution)/shard_map/ppermute | solution.py:23
  220.1 12.2 %collective-permute-done.23.refs_8_.refs_4_ = bf16[128,2048]{1,0:T(8,128)(2,1)S(1)} collective-permute-done((bf16[128,2048]{1,0:T(8,128)(2,1)S(1)}, bf16[128,2048]{1,0:T(8,128)(2,1)S(1)}, u32[]{:S(2)}, u32[]{:S(2)}) %collective-permute-start.23) | collective-permute-done | bytes 524320 | tf_op jit(solution)/shard_map/ppermute | solution.py:23
  232.3 10.8 %collective-permute-done.25.refs_10_.refs_6_ = bf16[128,2048]{1,0:T(8,128)(2,1)S(1)} collective-permute-done((bf16[128,2048]{1,0:T(8,128)(2,1)S(1)}, bf16[128,2048]{1,0:T(8,128)(2,1)S(1)}, u32[]{:S(2)}, u32[]{:S(2)}) %collective-permute-start.25) | collective-permute-done | bytes 524320 | tf_op jit(solution)/shard_map/ppermute | solution.py:23
  245.8 8.5 %collective-permute-done.18.refs_3_ = bf16[4,128,2176]{2,1,0:T(8,128)(2,1)} collective-permute-done((bf16[4,128,2176]{2,1,0:T(8,128)(2,1)}, bf16[4,128,2176]{2,1,0:T(8,128)(2,1)}, u32[]{:S(2)}, u32[]{:S(2)}) %collective-permute-start.18) | collective-permute-done | bytes 2228256 | tf_op jit(solution)/shard_map/ppermute | solution.py:43
  254.4 31.3 %feed.1 = (bf16[4,128,2048]{2,1,0:T(8,128)(2,1)}, bf16[4,128,2048]{2,1,0:T(8,128)(2,1)}, bf16[4,256,768]{2,1,0:T(8,128)(2,1)}, bf16[4,256,1408]{2,1,0:T(8,128)(2,1)}, bf16[4,128,2176]{2,1,0:T(8,128)(2,1)}) custom-call(s32[4]{0:T(128)} %copy-done.46, bf16[4,128,2176]{2,1,0:T(8,128)(2,1)} %all-to-all-done.refs_0_, ...), custom_call_target="tpu_custom_call" | custom-call | flops 14763950080 | bytes 12582912 | tf_op jit(solution)/shard_map/feed/pallas_call | solution.py:336
  294.6 14.2 %weight_grads.3 = (bf16[4,128,2176]{2,1,0:T(8,128)(2,1)}, bf16[4,128,2176]{2,1,0:T(8,128)(2,1)}, bf16[4,128,2176]{2,1,0:T(8,128)(2,1)}) custom-call(bf16[128,2048]{1,0:T(8,128)(2,1)} %copy-done.26, bf16[128,2048]{1,0:T(8,128)(2,1)} %copy-done.39, bf16[128,2048]{1,0:T(8,128)(2,1)} %copy-done.31, bf16[128,2048]{1,0:T(8,128)(2,1)} %copy-done.40, ...), custom_call_target="tpu_custom_call" | custom-call | flops 6845104128 | bytes 3145728 | tf_op jit(solution)/shard_map/weight_grads/pallas_call | solution.py:448
  312.5 25.5 %collective-permute-done.36 = bf16[4,128,2176]{2,1,0:T(8,128)(2,1)} collective-permute-done((bf16[4,128,2176]{2,1,0:T(8,128)(2,1)}, bf16[4,128,2176]{2,1,0:T(8,128)(2,1)}, u32[]{:S(2)}, u32[]{:S(2)}) %collective-permute-start.36) | collective-permute-done | bytes 2228256 | tf_op jit(solution)/shard_map/ppermute | solution.py:43
  347.7 10.5 %collective-permute-done.37.refs_6_.refs_10_ = bf16[128,2048]{1,0:T(8,128)(2,1)S(1)} collective-permute-done((bf16[128,2048]{1,0:T(8,128)(2,1)}, bf16[128,2048]{1,0:T(8,128)(2,1)S(1)}, u32[]{:S(2)}, u32[]{:S(2)}) %collective-permute-start.37) | collective-permute-done | bytes 524320 | tf_op jit(solution)/shard_map/ppermute | solution.py:23
  359.9 9.0 %feed_out.1 = (bf16[4,128,2048]{2,1,0:T(8,128)(2,1)}, bf16[4,128,2048]{2,1,0:T(8,128)(2,1)}) custom-call(s32[4]{0:T(128)} %copy-done.46, bf16[4,256,768]{2,1,0:T(8,128)(2,1)} %get-tuple-element.91.hidden.refs_17_, bf16[4,128,2176]{2,1,0:T(8,128)(2,1)} %all-to-all-done.refs_0_, bf16[4,128,2176]{2,1,0:T(8,128)(2,1)} %collective-permute-done.16.refs_1_, ...), custom_call_target="tpu_custom_call" | custom-call | flops 2952790016 | bytes 8388608 | tf_op jit(solution)/shard_map/feed_out/pallas_call | solution.py:382
  371.0 22.4 %collective-permute-done.39 = bf16[4,128,2176]{2,1,0:T(8,128)(2,1)} collective-permute-done((bf16[4,128,2176]{2,1,0:T(8,128)(2,1)}, bf16[4,128,2176]{2,1,0:T(8,128)(2,1)}, u32[]{:S(2)}, u32[]{:S(2)}) %collective-permute-start.39) | collective-permute-done | bytes 2228256 | tf_op jit(solution)/shard_map/ppermute | solution.py:43
  400.8 18.5 %attend_back.1 = (bf16[4,256,768]{2,1,0:T(8,128)(2,1)}, bf16[4,128,2048]{2,1,0:T(8,128)(2,1)}, bf16[4,128,2048]{2,1,0:T(8,128)(2,1)}) custom-call(s32[4]{0:T(128)} %copy-done.46, f32[4,256,128]{2,1,0:T(8,128)} %pad_maximum_fusion.cosine, f32[4,256,128]{2,1,0:T(8,128)} %pad_maximum_fusion.1.sine, bf16[4,256,256]{2,1,0:T(8,128)(2,1)} %and_convert_fusion.mask, ...), custom_call_target="tpu_custom_call" | custom-call | flops 4966055936 | bytes 8388608 | tf_op jit(solution)/shard_map/attend_back/pallas_call | solution.py:580
  440.1 8.3 %weight_grads.5 = (bf16[4,128,512]{2,1,0:T(8,128)(2,1)}, bf16[4,128,512]{2,1,0:T(8,128)(2,1)}, bf16[4,128,512]{2,1,0:T(8,128)(2,1)}, bf16[4,128,512]{2,1,0:T(8,1...) custom-call(bf16[128,2048]{1,0:T(8,128)(2,1)} %copy-done.3, bf16[128,2048]{1,0:T(8,128)(2,1)} %copy-done.12, ...), custom_call_target="tpu_custom_call" | custom-call | flops 3221225472 | bytes 3145728 | tf_op jit(solution)/shard_map/weight_grads/pallas_call | solution.py:448
  459.5 9.3 %collective-permute-done.47 = bf16[128,2048]{1,0:T(8,128)(2,1)S(1)} collective-permute-done((bf16[128,2048]{1,0:T(8,128)(2,1)S(1)}, bf16[128,2048]{1,0:T(8,128)(2,1)S(1)}, u32[]{:S(2)}, u32[]{:S(2)}) %collective-permute-start.47) | collective-permute-done | bytes 524320 | tf_op jit(solution)/shard_map/ppermute | solution.py:23
  495.9 8.5 %collective-permute-done.54 = bf16[4,128,512]{2,1,0:T(8,128)(2,1)} collective-permute-done((bf16[4,128,512]{2,1,0:T(8,128)(2,1)}, bf16[4,128,512]{2,1,0:T(8,128)(2,1)}, u32[]{:S(2)}, u32[]{:S(2)}) %collective-permute-start.54) | collective-permute-done | bytes 524320 | tf_op jit(solution)/shard_map/ppermute | solution.py:43
  512.1 11.4 %collective-permute-done.55 = bf16[4,128,512]{2,1,0:T(8,128)(2,1)} collective-permute-done((bf16[4,128,512]{2,1,0:T(8,128)(2,1)}, bf16[4,128,512]{2,1,0:T(8,128)(2,1)}, u32[]{:S(2)}, u32[]{:S(2)}) %collective-permute-start.55) | collective-permute-done | bytes 524320 | tf_op jit(solution)/shard_map/ppermute | solution.py:43
  (297 shorter events, 214.9 us)
Async XLA Ops:
  36.0 41.8 %all-to-all-start = ((bf16[4,128,2176]{2,1,0:T(8,128)(2,1)}), bf16[4,128,2176]{2,1,0:T(8,128)(2,1)}, u32[]{:S(2)}, u32[]{:S(2)}) async-start(bf16[4,128,2176]{2,1,0:T(8,128)(2,1)} %pack_feed.1), calls=%async_computation | async-start | bytes 4456448 | tf_op jit(solution)/shard_map/all_to_all | solution.py:90
  40.4 54.3 %collective-permute-start.4 = (bf16[128,2048]{1,0:T(8,128)(2,1)S(1)}, bf16[128,2048]{1,0:T(8,128)(2,1)S(1)}, u32[]{:S(2)}, u32[]{:S(2)}) collective-permute-start(bf16[128,2048]{1,0:T(8,128)(2,1)S(1)} %multiply_convert_fusion.1.refs_4_.refs_0_), channel_id=1, source_target_pairs={{0,1},{1,0},{2,3},{3,2},{4,5},{5,4},{6,7},{7,6},{8,9},{9,8},{10,11... | collective-permute-start | bytes 1572872 | tf_op jit(solution)/shard_map/ppermute | solution.py:27
  40.5 36.9 %collective-permute-start.6 = (bf16[128,2048]{1,0:T(8,128)(2,1)S(1)}, bf16[128,2048]{1,0:T(8,128)(2,1)S(1)}, u32[]{:S(2)}, u32[]{:S(2)}) collective-permute-start(bf16[128,2048]{1,0:T(8,128)(2,1)S(1)} %multiply_convert_fusion.1.refs_4_.refs_0_), channel_id=1, source_target_pairs={{0,4},{2,6},{4,0},{6,2},{8,12},{10,14},{12,8},{14,10},{16,20},{18,... | collective-permute-start | bytes 1572872 | tf_op jit(solution)/shard_map/ppermute | solution.py:23
  50.2 28.7 %collective-permute-start.2 = (bf16[4,128,1024]{2,1,0:T(8,128)(2,1)}, bf16[4,128,1024]{2,1,0:T(8,128)(2,1)}, u32[]{:S(2)}, u32[]{:S(2)}) collective-permute-start(bf16[4,128,1024]{2,1,0:T(8,128)(2,1)} %collective-permute-done.1.refs_1_), channel_id=1, source_target_pairs={{0,8},{2,10},{4,12},{6,14},{8,24},{10,26},{12,28},{14,30},{24,16},... | collective-permute-start | bytes 3145736 | tf_op jit(solution)/shard_map/ppermute | solution.py:43
  50.4 45.8 %collective-permute-start.5 = (bf16[128,2048]{1,0:T(8,128)(2,1)S(1)}, bf16[128,2048]{1,0:T(8,128)(2,1)}, u32[]{:S(2)}, u32[]{:S(2)}) collective-permute-start(bf16[128,2048]{1,0:T(8,128)(2,1)S(1)} %collective-permute-done.refs_6_.refs_2_), channel_id=1, source_target_pairs={{0,1},{1,0},{2,3},{3,2},{4,5},{5,4},{6,7},{7,6},{8,9},{9,8},{10,11... | collective-permute-start | bytes 1572872 | tf_op jit(solution)/shard_map/ppermute | solution.py:27
  78.8 27.3 %collective-permute-start.3 = (bf16[4,128,1024]{2,1,0:T(8,128)(2,1)}, bf16[4,128,1024]{2,1,0:T(8,128)(2,1)}, u32[]{:S(2)}, u32[]{:S(2)}) collective-permute-start(bf16[4,128,1024]{2,1,0:T(8,128)(2,1)} %collective-permute-done.2.refs_2_), channel_id=1, source_target_pairs={{0,8},{2,10},{4,12},{6,14},{8,24},{10,26},{12,28},{14,30},{24,16},... | collective-permute-start | bytes 3145736 | tf_op jit(solution)/shard_map/ppermute | solution.py:43
  94.8 58.3 %collective-permute-start.16 = (bf16[4,128,2176]{2,1,0:T(8,128)(2,1)}, bf16[4,128,2176]{2,1,0:T(8,128)(2,1)}, u32[]{:S(2)}, u32[]{:S(2)}) collective-permute-start(bf16[4,128,2176]{2,1,0:T(8,128)(2,1)} %all-to-all-done.refs_0_), channel_id=1, source_target_pairs={{0,8},{2,10},{4,12},{6,14},{8,24},{10,26},{12,28},{14,30},{24,16},... | collective-permute-start | bytes 6684680 | tf_op jit(solution)/shard_map/ppermute | solution.py:43
  121.9 38.4 %collective-permute-start.10 = (bf16[4,128,2048]{2,1,0:T(8,128)(2,1)}, bf16[4,128,2048]{2,1,0:T(8,128)(2,1)}, u32[]{:S(2)}, u32[]{:S(2)}) collective-permute-start(bf16[4,128,2048]{2,1,0:T(8,128)(2,1)} %get-tuple-element.81), channel_id=1, source_target_pairs={{0,1},{1,0},{2,3},{3,2},{4,5},{5,4},{6,7},{7,6},{8,9},{9,8},{10,11... | collective-permute-start | bytes 6291464 | tf_op jit(solution)/shard_map/ppermute | solution.py:27
  153.1 51.3 %collective-permute-start.17 = (bf16[4,128,2176]{2,1,0:T(8,128)(2,1)}, bf16[4,128,2176]{2,1,0:T(8,128)(2,1)}, u32[]{:S(2)}, u32[]{:S(2)}) collective-permute-start(bf16[4,128,2176]{2,1,0:T(8,128)(2,1)} %collective-permute-done.16.refs_1_), channel_id=1, source_target_pairs={{0,8},{2,10},{4,12},{6,14},{8,24},{10,26},{12,28},{14,30},{24,16},... | collective-permute-start | bytes 6684680 | tf_op jit(solution)/shard_map/ppermute | solution.py:43
  173.2 31.3 %collective-permute-start.15 = (bf16[128,2048]{1,0:T(8,128)(2,1)S(1)}, bf16[128,2048]{1,0:T(8,128)(2,1)S(1)}, u32[]{:S(2)}, u32[]{:S(2)}) collective-permute-start(bf16[128,2048]{1,0:T(8,128)(2,1)S(1)} %get-tuple-element.86), channel_id=1, source_target_pairs={{0,4},{2,6},{4,0},{6,2},{8,12},{10,14},{12,8},{14,10},{16,20},{18,... | collective-permute-start | bytes 1572872 | tf_op jit(solution)/shard_map/ppermute | solution.py:23
  204.4 50.0 %collective-permute-start.18 = (bf16[4,128,2176]{2,1,0:T(8,128)(2,1)}, bf16[4,128,2176]{2,1,0:T(8,128)(2,1)}, u32[]{:S(2)}, u32[]{:S(2)}) collective-permute-start(bf16[4,128,2176]{2,1,0:T(8,128)(2,1)} %collective-permute-done.17.refs_2_), channel_id=1, source_target_pairs={{0,8},{2,10},{4,12},{6,14},{8,24},{10,26},{12,28},{14,30},{24,16},... | collective-permute-start | bytes 6684680 | tf_op jit(solution)/shard_map/ppermute | solution.py:43
  285.8 52.2 %collective-permute-start.36 = (bf16[4,128,2176]{2,1,0:T(8,128)(2,1)}, bf16[4,128,2176]{2,1,0:T(8,128)(2,1)}, u32[]{:S(2)}, u32[]{:S(2)}) collective-permute-start(bf16[4,128,2176]{2,1,0:T(8,128)(2,1)} %get-tuple-element.99), channel_id=1, source_target_pairs={{0,8},{2,10},{4,12},{6,14},{8,24},{10,26},{12,28},{14,30},{24,16},... | collective-permute-start | bytes 6684680 | tf_op jit(solution)/shard_map/ppermute | solution.py:43
  310.4 31.8 %collective-permute-start.35 = (bf16[128,2048]{1,0:T(8,128)(2,1)S(1)}, bf16[128,2048]{1,0:T(8,128)(2,1)S(1)}, u32[]{:S(2)}, u32[]{:S(2)}) collective-permute-start(bf16[128,2048]{1,0:T(8,128)(2,1)S(1)} %get-tuple-element.98), channel_id=1, source_target_pairs={{0,4},{2,6},{4,0},{6,2},{8,12},{10,14},{12,8},{14,10},{16,20},{18,... | collective-permute-start | bytes 1572872 | tf_op jit(solution)/shard_map/ppermute | solution.py:23
  310.8 31.4 %collective-permute-start.34 = (bf16[128,2048]{1,0:T(8,128)(2,1)S(1)}, bf16[128,2048]{1,0:T(8,128)(2,1)S(1)}, u32[]{:S(2)}, u32[]{:S(2)}) collective-permute-start(bf16[128,2048]{1,0:T(8,128)(2,1)S(1)} %fusion), channel_id=1, source_target_pairs={{0,2},{2,0},{4,6},{6,4},{8,10},{10,8},{12,14},{14,12},{16,18},{18,... | collective-permute-start | bytes 1572872 | tf_op jit(solution)/shard_map/ppermute | solution.py:23
  342.2 51.2 %collective-permute-start.39 = (bf16[4,128,2176]{2,1,0:T(8,128)(2,1)}, bf16[4,128,2176]{2,1,0:T(8,128)(2,1)}, u32[]{:S(2)}, u32[]{:S(2)}) collective-permute-start(bf16[4,128,2176]{2,1,0:T(8,128)(2,1)} %add_convert_fusion.2), channel_id=1, source_target_pairs={{0,8},{2,10},{4,12},{6,14},{8,24},{10,26},{12,28},{14,30},{24,16},... | collective-permute-start | bytes 6684680 | tf_op jit(solution)/shard_map/ppermute | solution.py:43
  368.9 51.0 %collective-permute-start.33 = (bf16[4,128,2048]{2,1,0:T(8,128)(2,1)}, bf16[4,128,2048]{2,1,0:T(8,128)(2,1)}, u32[]{:S(2)}, u32[]{:S(2)}) collective-permute-start(bf16[4,128,2048]{2,1,0:T(8,128)(2,1)} %get-tuple-element.93), channel_id=1, source_target_pairs={{0,1},{1,0},{2,3},{3,2},{4,5},{5,4},{6,7},{7,6},{8,9},{9,8},{10,11... | collective-permute-start | bytes 6291464 | tf_op jit(solution)/shard_map/ppermute | solution.py:27
  369.0 28.6 %collective-permute-start.40 = (bf16[128,2048]{1,0:T(8,128)(2,1)}, bf16[128,2048]{1,0:T(8,128)(2,1)S(1)}, u32[]{:S(2)}, u32[]{:S(2)}) collective-permute-start(bf16[128,2048]{1,0:T(8,128)(2,1)} %get-tuple-element.100.refs_4_.refs_8_), channel_id=1, source_target_pairs={{0,1},{1,0},{2,3},{3,2},{4,5},{5,4},{6,7},{7,6},{8,9},{9,8},{10,11... | collective-permute-start | bytes 1572872 | tf_op jit(solution)/shard_map/ppermute | solution.py:27
  369.5 28.3 %collective-permute-start.41 = (bf16[128,2048]{1,0:T(8,128)(2,1)S(1)}, bf16[128,2048]{1,0:T(8,128)(2,1)S(1)}, u32[]{:S(2)}, u32[]{:S(2)}) collective-permute-start(bf16[128,2048]{1,0:T(8,128)(2,1)S(1)} %collective-permute-done.37.refs_6_.refs_10_), channel_id=1, source_target_pairs={{0,1},{1,0},{2,3},{3,2},{4,5},{5,4},{6,7},{7,6},{8,9},{9,8},{10,11... | collective-permute-start | bytes 1572872 | tf_op jit(solution)/shard_map/ppermute | solution.py:27
  371.0 27.4 %collective-permute-start.43 = (bf16[128,2048]{1,0:T(8,128)(2,1)}, bf16[128,2048]{1,0:T(8,128)(2,1)S(1)}, u32[]{:S(2)}, u32[]{:S(2)}) collective-permute-start(bf16[128,2048]{1,0:T(8,128)(2,1)} %collective-permute-done.42.refs_8_.refs_12_), channel_id=1, source_target_pairs={{0,1},{1,0},{2,3},{3,2},{4,5},{5,4},{6,7},{7,6},{8,9},{9,8},{10,11... | collective-permute-start | bytes 1572872 | tf_op jit(solution)/shard_map/ppermute | solution.py:27
  397.6 52.3 %collective-permute-start.52 = (bf16[4,128,2176]{2,1,0:T(8,128)(2,1)}, bf16[4,128,2176]{2,1,0:T(8,128)(2,1)}, u32[]{:S(2)}, u32[]{:S(2)}) collective-permute-start(bf16[4,128,2176]{2,1,0:T(8,128)(2,1)} %add_convert_fusion.1), channel_id=1, source_target_pairs={{0,8},{2,10},{4,12},{6,14},{8,24},{10,26},{12,28},{14,30},{24,16},... | collective-permute-start | bytes 6684680 | tf_op jit(solution)/shard_map/ppermute | solution.py:43
  419.4 31.3 %collective-permute-start.46 = (bf16[4,128,2048]{2,1,0:T(8,128)(2,1)}, bf16[4,128,2048]{2,1,0:T(8,128)(2,1)}, u32[]{:S(2)}, u32[]{:S(2)}) collective-permute-start(bf16[4,128,2048]{2,1,0:T(8,128)(2,1)} %get-tuple-element.111), channel_id=1, source_target_pairs={{0,1},{1,0},{2,3},{3,2},{4,5},{5,4},{6,7},{7,6},{8,9},{9,8},{10,11... | collective-permute-start | bytes 6291464 | tf_op jit(solution)/shard_map/ppermute | solution.py:27
  476.7 30.8 %collective-permute-start.49 = (bf16[128,2048]{1,0:T(8,128)(2,1)}, bf16[128,2048]{1,0:T(8,128)(2,1)}, u32[]{:S(2)}, u32[]{:S(2)}) collective-permute-start(bf16[128,2048]{1,0:T(8,128)(2,1)} %get-tuple-element.120), channel_id=1, source_target_pairs={{0,4},{2,6},{4,0},{6,2},{8,12},{10,14},{12,8},{14,10},{16,20},{18,... | collective-permute-start | bytes 1572872 | tf_op jit(solution)/shard_map/ppermute | solution.py:23
  478.4 29.1 %collective-permute-start.48 = (bf16[128,2048]{1,0:T(8,128)(2,1)}, bf16[128,2048]{1,0:T(8,128)(2,1)}, u32[]{:S(2)}, u32[]{:S(2)}) collective-permute-start(bf16[128,2048]{1,0:T(8,128)(2,1)} %add_convert_fusion.16), channel_id=1, source_target_pairs={{0,2},{2,0},{4,6},{6,4},{8,10},{10,8},{12,14},{14,12},{16,18},{18,... | collective-permute-start | bytes 1572872 | tf_op jit(solution)/shard_map/ppermute | solution.py:23
  483.3 42.2 %all-to-all-start.2 = ((bf16[4,128,2176]{2,1,0:T(8,128)(2,1)}), bf16[4,128,2176]{2,1,0:T(8,128)(2,1)}, u32[]{:S(2)}, u32[]{:S(2)}) async-start(bf16[4,128,2176]{2,1,0:T(8,128)(2,1)} %add_convert_fusion), calls=%async_computation.2 | async-start | bytes 4456448 | tf_op jit(solution)/shard_map/all_to_all | solution.py:90
  (89 other events, 1375.5 us)
